TPU v7x, 32 devices: a whole 2x2x4 slice. The times are simulated.
32 devices in a mesh: ctx: 4 (over y, core), db: 4 (over z), tp: 2 (over x).
Axes of the slice: x: 2, y: 2, z: 4, core: 2. Of those that a mesh axis runs over, the one named last changes fastest.
Arguments:
- hidden_in: bfloat16 [4, 1024, 4096], P('db', 'ctx', 'tp'), may hold values from -6 to 6
- queries: bfloat16 [4, 1024, 4096], P('db', 'ctx', 'tp')
- keys: bfloat16 [4, 1024, 4096], P('db', 'ctx', 'tp')
- values: bfloat16 [4, 1024, 4096], P('db', 'ctx', 'tp'), may hold values from -6 to 6
- cross_queries: bfloat16 [4, 1024, 4096], P('db', 'ctx', 'tp')
- neighbours: int32 [4, 16, 2], P('db', 'ctx'), may hold values from 0 to 31, as said below
- database: bfloat16 [2, 32, 128, 4096], P(None, 'db', None, 'tp')
- out_weight: bfloat16 [4096, 4096], P('tp', 'db'), may hold values from -0.125 to 0.125
Outputs:
- attended: bfloat16 [4, 1024, 4096], P('db', 'ctx', 'tp')
- mixed: bfloat16 [4, 1024, 4096], P('db', 'ctx', 'tp')
Inputs may be any that keep to these rules, and one draw needn't show every extreme that they name: `neighbours`: block id n is held by database shard n // 8. Among the 8 entries of the retrieval blocks of each aligned run of 256 positions of a sequence, no shard holds more than 4, and one shard holds exactly 4; in each such run of positions this shard is the same for all sequences.
All inputs are finite; a program needn't handle non-finite values.
Results may differ from a plain program's by a relative error of at most 0.007.
Values may be sent and summed in bfloat16 or wider, within the bound.
No kernel may reach another device: no remote copies, remote signals or barrier semaphores. Data moves between devices by JAX's collectives and lax.ppermute only.
A program may use at most 128 MiB of HBM per device.

v0:
```python
import math

import jax
import jax.numpy as jnp
from jax import lax
from jax.sharding import PartitionSpec as P

DH = 128
SPAN = 64


def passed_along(value, axis, steps):
    count = lax.axis_size(axis)
    leading, last = (max(0, -steps), min(count, count - steps))
    return lax.ppermute(value, axis, [(source, source + steps) for source in range(leading, last)])


def shards(hidden_in, queries, keys, values, cross_queries, neighbours, database, out_weight):
    rows_here = queries.shape[1]
    width_here = queries.shape[2]
    head_count = width_here // DH
    scale = 1.0 / math.sqrt(DH)
    member_count = lax.axis_size("ctx")
    member = lax.axis_index("ctx")
    row_index = jnp.arange(rows_here, dtype=jnp.int32)
    query_pos = member * rows_here + row_index

    def split_heads(array):
        return array[0].reshape(rows_here, head_count, DH).transpose(1, 0, 2)

    query_heads = split_heads(queries)
    moving_all = jnp.stack([split_heads(keys), split_heads(values)])

    def absorb(state, query_part, moving, source):
        best_so, total_so, accum_so = state
        key_pos = source * rows_here + row_index
        score = (
            jnp.einsum("hqd,hkd->hqk", query_part, moving[0], preferred_element_type=jnp.float32)
            * scale
        )
        allowed = (key_pos[None, :] <= query_pos[:, None])[None]
        peak = jnp.maximum(best_so, jnp.max(jnp.where(allowed, score, -1e30), axis=-1))
        weights = jnp.where(allowed, jnp.exp(score - peak[..., None]), 0.0)
        factor = jnp.exp(best_so - peak)
        total_new = total_so * factor + jnp.sum(weights, axis=-1)
        accum_new = accum_so * factor[..., None] + jnp.einsum(
            "hqk,hkd->hqd",
            weights.astype(jnp.bfloat16),
            moving[1],
            preferred_element_type=jnp.float32,
        )
        return (peak, total_new, accum_new)

    def advance(turn_index, carry):
        moving, state = carry
        state = absorb(state, query_heads, moving, (member - turn_index) % member_count)
        moving = passed_along(moving, "ctx", 1)
        return (moving, state)

    moving, state = lax.fori_loop(
        0,
        member_count - 1,
        advance,
        (
            moving_all,
            (
                jnp.full((head_count, rows_here), -1e30, jnp.float32),
                jnp.zeros((head_count, rows_here), jnp.float32),
                jnp.zeros((head_count, rows_here, DH), jnp.float32),
            ),
        ),
    )
    state = absorb(state, query_heads, moving, (member - member_count + 1) % member_count)
    total_final = state[1]
    accum_final = state[2]
    attended = (
        (accum_final / total_final[..., None])
        .astype(jnp.bfloat16)
        .transpose(1, 0, 2)
        .reshape(1, rows_here, width_here)
    )
    span_count = rows_here // SPAN
    entries = neighbours[0].reshape(-1)
    per_owner = database.shape[1]
    owner_count = lax.axis_size("db")
    slot_count = entries.shape[0] // 2
    owner_of = entries // per_owner
    local_of = entries % per_owner
    owner_hits = (owner_of[:, None] == jnp.arange(owner_count, dtype=jnp.int32)[None, :]).astype(
        jnp.int32
    )
    rank_of = jnp.sum((jnp.cumsum(owner_hits, axis=0) - owner_hits) * owner_hits, axis=1)
    place_of = owner_of * slot_count + rank_of
    place_hits = (
        place_of[:, None] == jnp.arange(owner_count * slot_count, dtype=jnp.int32)[None, :]
    ).astype(jnp.int32)
    request = jnp.sum(place_hits * local_of[:, None], axis=0).reshape(owner_count, slot_count)
    asked = lax.all_to_all(request, "db", split_axis=0, concat_axis=0, tiled=True)
    fetched = jnp.take(database, asked.reshape(-1), axis=1).reshape(
        2, owner_count, slot_count, database.shape[2], width_here
    )
    returned = lax.all_to_all(fetched, "db", split_axis=1, concat_axis=1, tiled=True)
    flat_rows = returned.reshape(2, owner_count * slot_count, database.shape[2], width_here)
    near_rows = jnp.take(flat_rows, place_of, axis=1).reshape(2, span_count, -1, head_count, DH)
    cross_heads = cross_queries[0].reshape(span_count, SPAN, head_count, DH)
    cross_score = (
        jnp.einsum("cqhd,ckhd->chqk", cross_heads, near_rows[0], preferred_element_type=jnp.float32)
        * scale
    )
    cross_peak = jnp.max(cross_score, axis=-1)
    cross_weights = jnp.exp(cross_score - cross_peak[..., None])
    cross_total = jnp.sum(cross_weights, axis=-1)
    cross_accum = jnp.einsum(
        "chqk,ckhd->cqhd",
        cross_weights.astype(jnp.bfloat16),
        near_rows[1],
        preferred_element_type=jnp.float32,
    )
    cross_out = (
        (cross_accum / cross_total.transpose(0, 2, 1)[..., None])
        .astype(jnp.bfloat16)
        .reshape(rows_here, width_here)
    )
    terms = jnp.dot(
        cross_out,
        lax.all_gather(out_weight, "db", axis=1, tiled=True),
        preferred_element_type=jnp.float32,
    )
    summed = lax.psum_scatter(
        terms.astype(jnp.bfloat16), "tp", scatter_dimension=1, tiled=True
    ).astype(jnp.float32)
    mixed = (
        (hidden_in[0].astype(jnp.float32) + summed)
        .astype(jnp.bfloat16)
        .reshape(1, rows_here, width_here)
    )
    return (attended, mixed)


def solution(mesh):
    in_specs = (
        P("db", "ctx", "tp"),
        P("db", "ctx", "tp"),
        P("db", "ctx", "tp"),
        P("db", "ctx", "tp"),
        P("db", "ctx", "tp"),
        P("db", "ctx", None),
        P(None, "db", None, "tp"),
        P("tp", "db"),
    )
    out_specs = (P("db", "ctx", "tp"), P("db", "ctx", "tp"))
    return jax.shard_map(shards, mesh=mesh, in_specs=in_specs, out_specs=out_specs, check_vma=False)
```

profile of v0, /device:TPU:1, one launch (start us, length us, event | category | flops | bytes accessed | tf_op | source)
XLA Modules:
  0.0 850.2 jit_solution(14015233464452294343)
XLA Ops:
  8.4 9.6 %all_to_all.14 = s32[4,1,4]{2,1,0:T(1,128)S(1)} all-to-all(s32[4,1,4]{2,1,0:T(1,128)S(1)} %bitcast.134), channel_id=1, replica_groups=mesh['ctx'=4,'db'=4,'tp'=2] {'db'}, dimensions={0} | all-to-all | bytes 128 | tf_op jit(solution)/shard_map/all_to_all | solution.py:98
  19.3 10.6 %gather_fusion = bf16[16,2,128,2048]{3,2,1,0:T(8,128)(2,1)} fusion(bf16[2,8,128,2048]{3,2,1,0:T(8,128)(2,1)} %param.16, s32[1024]{0:T(1024)S(1)} %pad_clamp_fusion.1), kind=kCustom, calls=%fused_computation | custom fusion | bytes 33554496 | tf_op jit(solution)/shard_map/jit(_take)/gather | solution.py:99
  29.9 8.1 copy.125
  40.2 6.5 copy.126
  46.7 7.0 all-to-all-start.1
  61.0 2.8 pad_maximum_fusion
  63.8 3.1 copy.117
  67.0 618.6 %all-to-all-done.1 = bf16[2,4,4,128,2048]{4,3,2,0,1:T(8,128)(2,1)} async-done(((bf16[2,4,4,128,2048]{4,3,2,0,1:T(8,128)(2,1)}), bf16[2,4,4,128,2048]{4,3,2,0,1:T(8,128)(2,1)}, u32[]{:S(2)}, u32[]{:S(2)}) %all-to-all-start.1) | async-done | bytes 16777248 | tf_op jit(solution)/shard_map/all_to_all | solution.py:102
  685.6 14.1 %copy.127 = bf16[2,4,4,128,2048]{4,3,2,1,0:T(8,128)(2,1)} copy(bf16[2,4,4,128,2048]{4,3,2,0,1:T(8,128)(2,1)} %all-to-all-done.1) | data formatting | bytes 33554432 | tf_op jit(solution)/shard_map/all_to_all | solution.py:102
  699.7 10.4 %gather_fusion.1 = bf16[8,2,128,2048]{3,2,1,0:T(8,128)(2,1)} fusion(bf16[2,16,128,2048]{3,2,1,0:T(8,128)(2,1)} %bitcast.119, s32[1024]{0:T(1024)S(1)} %pad_clamp_fusion), kind=kCustom, calls=%fused_computation.1 | custom fusion | bytes 16777248 | tf_op jit(solution)/shard_map/jit(_take)/gather | solution.py:104
  710.2 7.5 select_bitcast_fusion
  717.6 4.0 fusion.65
  731.4 12.0 %convolution_convert_fusion = bf16[256,4096]{1,0:T(8,128)(2,1)} fusion(bf16[2048,4096]{1,0:T(8,128)(2,1)} %all-gather.2.cloned.1.call-done, bf16[32,8,16,128]{3,2,1,0:T(8,128)(2,1)} %bitcast.131), kind=kOutput, calls=%fused_computation.31 | convolution fusion | flops 4296015872 | bytes 19922944 | tf_op jit(solution)/shard_map/dot_general | solution.py:124
  743.4 86.9 %while.22 = (s32[]{:T(128)}, bf16[2,16,256,128]{3,2,1,0:T(8,128)(2,1)S(1)}, f32[16,256]{1,0:T(8,128)S(1)}, f32[16,256]{1,0:T(8,128)S(1)}, f32[16,256,128]{2,1,0:...) while((s32[]{:T(128)}, ...), condition=%wide.region_3.4_spmd.clone, body=%wide.region_0.3_spmd.clone.sunk | while | flops 550064640 | bytes 49811796 | solution.py:60
  745.0 4.3 collective-permute-start
  754.5 5.4 fusion.80
  759.9 12.6 %collective-permute-done = bf16[2,16,256,128]{3,2,1,0:T(8,128)(2,1)S(1)} collective-permute-done((bf16[2,16,256,128]{3,2,1,0:T(8,128)(2,1)}, bf16[2,16,256,128]{3,2,1,0:T(8,128)(2,1)S(1)}, u32[]{:S(2)}, u32[]{:S(2)}) %collective-permute-start) | collective-permute-done | bytes 2097184 | tf_op jit(solution)/shard_map/while/body/eval_jaxpr/ppermute | solution.py:15
  773.8 4.3 collective-permute-start
  783.1 6.1 fusion.80
  789.3 12.1 %collective-permute-done = bf16[2,16,256,128]{3,2,1,0:T(8,128)(2,1)S(1)} collective-permute-done((bf16[2,16,256,128]{3,2,1,0:T(8,128)(2,1)}, bf16[2,16,256,128]{3,2,1,0:T(8,128)(2,1)S(1)}, u32[]{:S(2)}, u32[]{:S(2)}) %collective-permute-start) | collective-permute-done | bytes 2097184 | tf_op jit(solution)/shard_map/while/body/eval_jaxpr/ppermute | solution.py:15
  802.7 4.3 collective-permute-start
  812.0 6.1 fusion.80
  818.1 12.1 %collective-permute-done = bf16[2,16,256,128]{3,2,1,0:T(8,128)(2,1)S(1)} collective-permute-done((bf16[2,16,256,128]{3,2,1,0:T(8,128)(2,1)}, bf16[2,16,256,128]{3,2,1,0:T(8,128)(2,1)S(1)}, u32[]{:S(2)}, u32[]{:S(2)}) %collective-permute-start) | collective-permute-done | bytes 2097184 | tf_op jit(solution)/shard_map/while/body/eval_jaxpr/ppermute | solution.py:15
  832.9 2.9 copy.120
  (98 shorter events, 50.7 us)
Async XLA Ops:
  46.7 638.9 %all-to-all-start.1 = ((bf16[2,4,4,128,2048]{4,3,2,0,1:T(8,128)(2,1)}), bf16[2,4,4,128,2048]{4,3,2,0,1:T(8,128)(2,1)}, u32[]{:S(2)}, u32[]{:S(2)}) async-start(bf16[2,4,4,128,2048]{4,3,2,0,1:T(8,128)(2,1)} %copy.126), calls=%async_computation.1 | async-start | bytes 33554432 | tf_op jit(solution)/shard_map/all_to_all | solution.py:102
  53.7 1.2 copy-start.7
  53.7 2.4 copy-start.8
  53.7 677.8 %all-gather.2.cloned.1.call-start = ((), (), s32[]{:S(2)}) async-start(), calls=%async_computation.3 | async-start | bytes 20971520 | tf_op jit(solution)/shard_map/all_gather | solution.py:126
  54.4 786.3 %reduce-scatter.2.cloned.1.call-start = ((), (), s32[]{:S(2)}) async-start(), calls=%async_computation.4 | async-start | bytes 3145728 | tf_op jit(solution)/shard_map/reduce_scatter | solution.py:129
  56.6 4.4 copy-start.1
  723.1 1.4 copy-start.3
  745.0 27.5 %collective-permute-start = (bf16[2,16,256,128]{3,2,1,0:T(8,128)(2,1)}, bf16[2,16,256,128]{3,2,1,0:T(8,128)(2,1)S(1)}, u32[]{:S(2)}, u32[]{:S(2)}) collective-permute-start(bf16[2,16,256,128]{3,2,1,0:T(8,128)(2,1)} %copy.163), channel_id=1, source_target_pairs={{0,8},{8,16},{16,24},{1,9},{9,17},{17,25},{2,10},{10,18},{18,26},{... | collective-permute-start | bytes 6291464 | tf_op jit(solution)/shard_map/while/body/eval_jaxpr/ppermute | solution.py:15
  751.6 1.9 copy-start
  773.8 27.6 %collective-permute-start = (bf16[2,16,256,128]{3,2,1,0:T(8,128)(2,1)}, bf16[2,16,256,128]{3,2,1,0:T(8,128)(2,1)S(1)}, u32[]{:S(2)}, u32[]{:S(2)}) collective-permute-start(bf16[2,16,256,128]{3,2,1,0:T(8,128)(2,1)} %copy.163), channel_id=1, source_target_pairs={{0,8},{8,16},{16,24},{1,9},{9,17},{17,25},{2,10},{10,18},{18,26},{... | collective-permute-start | bytes 6291464 | tf_op jit(solution)/shard_map/while/body/eval_jaxpr/ppermute | solution.py:15
  780.3 1.9 copy-start
  802.7 27.6 %collective-permute-start = (bf16[2,16,256,128]{3,2,1,0:T(8,128)(2,1)}, bf16[2,16,256,128]{3,2,1,0:T(8,128)(2,1)S(1)}, u32[]{:S(2)}, u32[]{:S(2)}) collective-permute-start(bf16[2,16,256,128]{3,2,1,0:T(8,128)(2,1)} %copy.163), channel_id=1, source_target_pairs={{0,8},{8,16},{16,24},{1,9},{9,17},{17,25},{2,10},{10,18},{18,26},{... | collective-permute-start | bytes 6291464 | tf_op jit(solution)/shard_map/while/body/eval_jaxpr/ppermute | solution.py:15
  809.2 1.9 copy-start
  830.3 5.7 copy-start.2
  835.9 1.8 copy-start.4
  836.0 2.2 copy-start.5
  838.2 2.6 copy-start.6
Sparse Core Ops, SparseCore 0:
  56.1 586.8 all-gather.1
  743.5 31.4 reduce-scatter.1
where the time goes:
time: 851 us; the launch traced here: 850 us
  waiting for transfers between devices  656 us (77%)
  local copies, waits for them, and re-layouts  86.6 us (10%)
  matrix products  41.7 us (5%)
  other arithmetic  21.4 us (3%)
  starting transfers between devices  19.8 us (2%)
  between operations  14.3 us (2%)
  blocking collectives  9.61 us (1%)
    all_to_all x1, waiting for transfers between devices, shards(): lax.all_to_all(fetched, 'db', split_axis=1, concat_axis=1, tiled=True)  619 us
    ppermute x3, waiting for transfers between devices, passed_along(): lax.ppermute(value, axis, [(source, source + steps) for source in range(l...  36.9 us
    dot_general x4, matrix products, absorb(): jnp.einsum('hqk,hkd->hqd', weights.astype(jnp.bfloat16), moving[1], prefe...  18.9 us
    gather x2, local copies, waits for them, and re-layouts, shards(): jnp.take(database, asked.reshape(-1), axis=1)  18.7 us
  transfers between devices with their start and end apart: 6, of which 4 were waited for; matrix products, arithmetic and copies ran while one was open for 12% of the time, Pallas kernels for 0%

commit v1 on v0

v1 whole, which is shorter than its diff:
```python
import functools
import math

import jax
import jax.numpy as jnp
from jax import lax
from jax.experimental import pallas as pl
from jax.experimental.pallas import tpu as pltpu
from jax.sharding import PartitionSpec as P

DH = 128
SPAN = 64
LANES = 128
NEG = -1e30
FLOOR = -1e29
SCALE2 = math.log2(math.e) / math.sqrt(DH)
VMEM_BYTES = 48 * 1024 * 1024

PAIR = [(0, 1), (1, 0), (2, 3), (3, 2)]
MIDDLE = [(1, 2), (2, 1)]
INWARD = [(0, 1), (3, 2)]
OUTWARD = [(1, 0), (2, 3)]


def scores(query, key):
    return (
        lax.dot_general(query, key, (((1,), (1,)), ((), ())), preferred_element_type=jnp.float32)
        * SCALE2
    )


def self_kernel(flags, q_ref, k_ref, v_ref, *rest, group, blocks, rows):
    others, (out_ref, peak_ref, total_ref, accum_ref) = rest[:-4], rest[-4:]
    row = lax.broadcasted_iota(jnp.int32, (rows, rows), 0)
    col = lax.broadcasted_iota(jnp.int32, (rows, rows), 1)
    for g in range(group):
        cols = slice(g * DH, (g + 1) * DH)
        score = jnp.where(col <= row, scores(q_ref[:, cols], k_ref[:, cols]), NEG)
        peak = jnp.max(score, axis=-1, keepdims=True)
        weights = jnp.exp2(score - peak)
        total = jnp.sum(weights, axis=-1, keepdims=True)
        accum_ref[g] = jnp.dot(
            weights.astype(jnp.bfloat16), v_ref[:, cols], preferred_element_type=jnp.float32
        )
        peak_ref[g] = jnp.broadcast_to(peak, (rows, LANES))
        total_ref[g] = jnp.broadcast_to(total, (rows, LANES))
    for index, (operand, start) in enumerate(blocks):

        @pl.when(flags[index] == 1)
        def _(operand=operand, start=start):
            key_ref, value_ref = others[2 * operand], others[2 * operand + 1]
            for g in range(group):
                cols = slice(g * DH, (g + 1) * DH)
                score = scores(q_ref[:, cols], key_ref[start : start + rows, cols])
                before = peak_ref[g][:, :1]
                peak = jnp.maximum(before, jnp.max(score, axis=-1, keepdims=True))
                weights = jnp.exp2(score - peak)
                factor = jnp.exp2(before - peak)
                total = total_ref[g][:, :1] * factor + jnp.sum(weights, axis=-1, keepdims=True)
                accum_ref[g] = accum_ref[g] * factor + jnp.dot(
                    weights.astype(jnp.bfloat16),
                    value_ref[start : start + rows, cols],
                    preferred_element_type=jnp.float32,
                )
                peak_ref[g] = jnp.broadcast_to(peak, (rows, LANES))
                total_ref[g] = jnp.broadcast_to(total, (rows, LANES))

    for g in range(group):
        cols = slice(g * DH, (g + 1) * DH)
        out_ref[:, cols] = (accum_ref[g] / total_ref[g][:, :1]).astype(jnp.bfloat16)


def self_attention(flags, queries, keys, values, others, blocks):
    rows, width = queries.shape
    heads = width // DH
    group = math.gcd(heads, 4)

    def spec(array):
        return pl.BlockSpec((array.shape[0], group * DH), lambda h, flags: (0, h))

    operands = [queries, keys, values] + [array for pair in others for array in pair]
    pairs = (len(blocks) + 1) * rows * rows * heads
    return pl.pallas_call(
        functools.partial(self_kernel, group=group, blocks=blocks, rows=rows),
        out_shape=jax.ShapeDtypeStruct((rows, width), jnp.bfloat16),
        grid_spec=pltpu.PrefetchScalarGridSpec(
            num_scalar_prefetch=1,
            grid=(heads // group,),
            in_specs=[spec(array) for array in operands],
            out_specs=spec(queries),
            scratch_shapes=[
                pltpu.VMEM((group, rows, LANES), jnp.float32),
                pltpu.VMEM((group, rows, LANES), jnp.float32),
                pltpu.VMEM((group, rows, DH), jnp.float32),
            ],
        ),
        compiler_params=pltpu.CompilerParams(vmem_limit_bytes=VMEM_BYTES),
        cost_estimate=pl.CostEstimate(
            flops=4 * pairs * DH,
            bytes_accessed=sum(array.size * 2 for array in operands) + rows * width * 2,
            transcendentals=pairs,
        ),
        name="self_attention",
    )(flags, *operands)


def cross_kernel(meta, *refs, base, heads, group, span_count, near, two_queries, states, final):
    refs = list(refs)
    query_refs = [refs.pop(0) for _ in range(1 + two_queries)]
    database_ref = refs.pop(0)
    state_refs = [(refs.pop(0), refs.pop(0)) for _ in range(states)]
    out_ref = refs.pop(0)
    step = pl.program_id(0)
    width = heads * DH
    length = database_ref.shape[2]

    @pl.when(meta[base] == 1)
    def _():
        lane = lax.broadcasted_iota(jnp.int32, (SPAN, LANES), 1)
        for u in range(span_count):
            rows = slice(u * SPAN, (u + 1) * SPAN)
            places = [meta[base + 5 + u * near + n] for n in range(near)]
            stats = [
                jnp.where(meta[base + 3 + i] == 1, 1.0, 0.0) * ref[rows, :].astype(jnp.float32)
                for i, (_, ref) in enumerate(state_refs)
            ]
            coded = jnp.zeros((SPAN, LANES), jnp.float32)
            for g in range(group):
                cols = slice(g * DH, (g + 1) * DH)
                head = step * group + g
                mine = (lane == head) | (lane == heads + head) | (lane == 2 * heads + head)
                query = query_refs[0][rows, cols]
                if two_queries:
                    query = jnp.where(meta[base + 1] == 1, query, query_refs[1][rows, cols])
                found = []
                for place in places:
                    key = database_ref[0, jnp.maximum(place, 0), :, cols]
                    found.append(jnp.where(place >= 0, scores(query, key), NEG))
                came = []
                for i in range(states):
                    level = jnp.sum(jnp.where(mine, stats[i], 0.0), axis=-1, keepdims=True)
                    came.append(jnp.where(meta[base + 3 + i] == 1, level, NEG))
                peak = jnp.full((SPAN, 1), FLOOR, jnp.float32)
                for score in found:
                    peak = jnp.maximum(peak, jnp.max(score, axis=-1, keepdims=True))
                for level in came:
                    peak = jnp.maximum(peak, level)
                total = jnp.zeros((SPAN, 1), jnp.float32)
                accum = jnp.zeros((SPAN, DH), jnp.float32)
                for place, score in zip(places, found):
                    weights = jnp.exp2(score - peak)
                    total += jnp.sum(weights, axis=-1, keepdims=True)
                    accum += jnp.dot(
                        weights.astype(jnp.bfloat16),
                        database_ref[1, jnp.maximum(place, 0), :, cols],
                        preferred_element_type=jnp.float32,
                    )
                for i, level in enumerate(came):
                    factor = jnp.exp2(level - peak)
                    total += factor
                    accum += factor * jnp.where(
                        meta[base + 3 + i] == 1,
                        state_refs[i][0][rows, cols].astype(jnp.float32),
                        0.0,
                    )
                some = total > 0.0
                safe = jnp.where(some, total, 1.0)
                result = (accum / safe).astype(jnp.bfloat16)
                if final:
                    out_ref[rows, cols] = result
                    continue
                at = pl.multiple_of(step * (group * DH) + g * DH, DH)
                out_ref[rows, pl.ds(at, DH)] = result
                level = jnp.where(some, peak + jnp.log2(safe), NEG)
                high = level.astype(jnp.bfloat16).astype(jnp.float32)
                mid = (level - high).astype(jnp.bfloat16).astype(jnp.float32)
                low = level - high - mid
                coded += jnp.where(
                    lane == head,
                    high,
                    jnp.where(
                        lane == heads + head, mid, jnp.where(lane == 2 * heads + head, low, 0.0)
                    ),
                )
            if not final:
                before = jnp.where(step == 0, 0.0, 1.0) * jnp.where(
                    step == 0, 0.0, out_ref[rows, width:].astype(jnp.float32)
                )
                out_ref[rows, width:] = (before + coded).astype(jnp.bfloat16)


def cross_attention(meta, base, queries, database, states, final):
    rows, width = queries[0].shape
    heads = width // DH
    group = math.gcd(heads, 4)
    wide = group * DH
    near = (meta.shape[1] - 5) // (rows // SPAN)
    span_count = rows // SPAN
    at = base * meta.shape[1]
    per_owner, length = database.shape[1], database.shape[2]
    in_specs = [
        pl.BlockSpec((rows, wide), lambda h, meta, i=i: (0, h * meta[at + 1 + i]))
        for i in range(len(queries))
    ]
    in_specs.append(
        pl.BlockSpec(
            (2, per_owner, length, wide), lambda h, meta: (0, 0, 0, h * meta[at])
        )
    )
    operands = [*queries, database]
    for i, state in enumerate(states):
        in_specs.append(pl.BlockSpec((rows, wide), lambda h, meta, i=i: (0, h * meta[at + 3 + i])))
        in_specs.append(pl.BlockSpec((rows, LANES), lambda h, meta: (0, heads)))
        operands += [state, state]
    if final:
        out_width = width
        out_spec = pl.BlockSpec((rows, wide), lambda h, meta: (0, h))
    else:
        out_width = width + LANES
        out_spec = pl.BlockSpec((rows, out_width), lambda h, meta: (0, 0))
    pairs = rows * near * length * heads
    return pl.pallas_call(
        functools.partial(
            cross_kernel,
            base=at,
            heads=heads,
            group=group,
            span_count=span_count,
            near=near,
            two_queries=len(queries) - 1,
            states=len(states),
            final=final,
        ),
        out_shape=jax.ShapeDtypeStruct((rows, out_width), jnp.bfloat16),
        grid_spec=pltpu.PrefetchScalarGridSpec(
            num_scalar_prefetch=1,
            grid=(heads // group,),
            in_specs=in_specs,
            out_specs=out_spec,
        ),
        compiler_params=pltpu.CompilerParams(vmem_limit_bytes=VMEM_BYTES),
        cost_estimate=pl.CostEstimate(
            flops=4 * pairs * DH,
            bytes_accessed=database.size * 2 + rows * width * 2 * (2 + len(states)),
            transcendentals=pairs,
        ),
        name="cross_attention",
    )(meta.reshape(-1), *operands)


def project_kernel(meta, x_ref, *refs, sides, depth, columns, tile):
    count = 1 + sum(len(side) for side in sides)
    weight_refs, (out_ref, held, sems) = refs[:count], refs[count:]
    own = [(weight_refs[0], 0, depth)]
    lists = []
    taken = 1
    for side in sides:
        lists.append(
            [
                (ref, offset if isinstance(offset, int) else meta[offset[0]], size)
                for ref, (offset, size) in zip(weight_refs[taken : taken + len(side)], side)
            ]
        )
        taken += len(side)

    def run(first, second):
        copies = []
        for slot, pieces in enumerate((first, second)):
            copies.append([])
            for index, (ref, offset, size) in enumerate(pieces):
                if not isinstance(offset, int):
                    offset = pl.multiple_of(offset, size)
                copy = pltpu.make_async_copy(
                    ref, held.at[slot, pl.ds(offset, size), :], sems.at[slot, index]
                )
                copy.start()
                copies[-1].append(copy)
        for slot in range(2):
            for copy in copies[slot]:
                copy.wait()

            @pl.loop(0, columns // tile)
            def _(n, slot=slot):
                part = pl.multiple_of(n * tile, tile)
                place = pl.multiple_of(meta[2 + slot] * columns + n * tile, tile)
                out_ref[:, pl.ds(place, tile)] = jnp.dot(
                    x_ref[...],
                    held[slot, :, pl.ds(part, tile)],
                    preferred_element_type=jnp.float32,
                ).astype(jnp.bfloat16)

    @pl.when((meta[0] == 1) & (meta[1] == 0))
    def _():
        run(own, lists[0])

    @pl.when((meta[0] == 1) & (meta[1] == 1))
    def _():
        run(lists[1], lists[2])


def project(meta, x, weight, sides):
    rows, depth = x.shape
    columns = weight.shape[1]
    operands = [weight] + [array for side in sides for array, _ in side]
    most = max(len(side) for side in sides)
    shapes = [[(offset, array.shape[0]) for array, offset in side] for side in sides]
    return pl.pallas_call(
        functools.partial(
            project_kernel, sides=shapes, depth=depth, columns=columns, tile=min(256, columns)
        ),
        out_shape=jax.ShapeDtypeStruct((rows, 2 * columns), jnp.bfloat16),
        in_specs=[pl.BlockSpec(memory_space=pltpu.SMEM), pl.BlockSpec(memory_space=pltpu.VMEM)]
        + [pl.BlockSpec(memory_space=pl.ANY)] * len(operands),
        out_specs=pl.BlockSpec(memory_space=pltpu.VMEM),
        scratch_shapes=[
            pltpu.VMEM((2, depth, columns), jnp.bfloat16),
            pltpu.SemaphoreType.DMA((2, most)),
        ],
        compiler_params=pltpu.CompilerParams(vmem_limit_bytes=VMEM_BYTES),
        cost_estimate=pl.CostEstimate(
            flops=4 * rows * depth * columns,
            bytes_accessed=4 * depth * columns + 2 * rows * (depth + 2 * columns),
            transcendentals=0,
        ),
        name="project",
    )(meta, x, *operands)


def after(value, *earlier):
    return lax.optimization_barrier((value, *earlier))[0]


def shards(hidden_in, queries, keys, values, cross_queries, neighbours, database, out_weight):
    rows, width = queries.shape[1:]
    member_count = lax.axis_size("ctx")
    part_count = lax.axis_size("tp")
    assert lax.axis_size("db") == 4
    member = lax.axis_index("ctx")
    plane = lax.axis_index("db")
    part = lax.axis_index("tp")
    outer = (plane == 0) | (plane == 3)
    inner = jnp.logical_not(outer)
    two_level = member_count == 4
    CORE = [(0, 1), (1, 0), (2, 3), (3, 2)]
    ACROSS = [(0, 2), (1, 3), (2, 0), (3, 1)]

    def send(value, perm, axis="db"):
        return lax.ppermute(value, axis, perm)

    query = cross_queries[0]
    ids = lax.all_gather(neighbours[0].reshape(-1), "db")
    query_a = send(query, PAIR)
    query_m = send(query, MIDDLE)

    key, value = keys[0], values[0]
    if two_level:
        key_y = send(key, [(0, 2), (1, 3)], "ctx")
        value_y = send(value, [(0, 2), (1, 3)], "ctx")
        key_c = send(key, [(0, 1), (2, 3)], "ctx")
        value_c = send(value, [(0, 1), (2, 3)], "ctx")
        key_yc = send(key_y, [(2, 3), (3, 2)], "ctx")
        value_yc = send(value_y, [(2, 3), (3, 2)], "ctx")
        flags = jnp.stack([member % 2, member // 2, member // 2]).astype(jnp.int32)
        others = [(key_c, value_c), (key_y, value_y), (key_yc, value_yc)]
        blocks = [(0, 0), (1, 0), (2, 0)]
    else:
        others = [
            (
                lax.all_gather(key, "ctx", axis=0, tiled=True),
                lax.all_gather(value, "ctx", axis=0, tiled=True),
            )
        ]
        blocks = [(0, j * rows) for j in range(member_count)]
        flags = (jnp.arange(member_count) < member).astype(jnp.int32)

    depth = out_weight.shape[0]
    share = depth // member_count
    own_share = lax.dynamic_slice_in_dim(out_weight, member * share, share, axis=0)
    query_c = send(query_a, MIDDLE)
    query_b_out = send(query_m, OUTWARD)
    share_a = send(after(own_share, query_a), INWARD)
    share_b = send(after(own_share, query_c), MIDDLE)
    share_c = send(after(share_a, share_b), MIDDLE)
    query_c_out = send(after(query_c, query_b_out), OUTWARD)

    def whole(piece):
        if not two_level:
            return [(lax.all_gather(piece, "ctx", axis=0, tiled=True), 0)]
        across = send(piece, ACROSS, "ctx")
        beside = send(piece, CORE, "ctx")
        corner = send(across, CORE, "ctx")
        return [(piece, (4,)), (across, (5,)), (beside, (6,)), (corner, (7,))]

    per_owner = database.shape[1]
    local = jnp.where(ids // per_owner == plane, ids % per_owner, -1)
    seq_a = plane ^ 1
    seq_b = jnp.where(plane < 2, 2, 1)
    seq_c = jnp.where(plane < 2, 3, 0)
    one = jnp.ones((), jnp.int32)
    zero = jnp.zeros((), jnp.int32)
    is_outer = outer.astype(jnp.int32)
    is_inner = inner.astype(jnp.int32)

    def described(active, first, second, state, other, seq):
        head = jnp.stack([active, first, second, state, other]).astype(jnp.int32)
        return jnp.concatenate([head, lax.dynamic_index_in_dim(local, seq, 0, keepdims=False)])

    meta = jnp.stack(
        [
            described(is_outer, is_outer, zero, zero, zero, plane),
            described(is_outer, is_outer, zero, zero, zero, seq_c),
            described(one, is_outer, is_inner, is_inner, zero, jnp.where(outer, seq_b, seq_c)),
            described(one, is_outer, is_inner, is_inner, zero, jnp.where(outer, seq_a, seq_b)),
            described(is_inner, is_inner, zero, is_inner, is_inner, seq_a),
            described(is_inner, is_inner, zero, is_inner, is_inner, plane),
        ]
    )

    def cross(call, call_queries, states=(), final=False):
        return cross_attention(meta, call, call_queries, database, states, final)

    own_part = send(after(cross(0, [query]), share_a), INWARD)
    in_1 = send(cross(1, [query_c_out]), INWARD)
    pieces_a, pieces_b, pieces_c = whole(share_a), whole(share_b), whole(share_c)
    part_2 = cross(2, [query_b_out, query_c], [in_1])
    in_2 = send(part_2, INWARD)
    mid_2 = send(part_2, MIDDLE)
    part_3 = cross(3, [query_a, query_m], [in_2])
    in_3 = send(part_3, INWARD)
    mid_3 = send(part_3, MIDDLE)
    cross_a = cross(4, [query_a], [mid_2, own_part], final=True)

    side = plane // 2
    offsets = [member * share, (member ^ 2) * share, (member ^ 1) * share, (member ^ 3) * share]

    def projected(x, half):
        group = jnp.where(side == half, 0, 1)
        first = jnp.where(group == 0, plane % 2, seq_b % 2)
        second = jnp.where(group == 0, seq_a % 2, seq_c % 2)
        numbers = jnp.stack([is_inner, group, first, second, *offsets]).astype(jnp.int32)
        return project(numbers, x, out_weight, [pieces_a, pieces_b, pieces_c])

    def reduced(x):
        if part_count != 2:
            both = jnp.concatenate([projected(x, 0), projected(x, 1)], axis=1)
            return lax.psum_scatter(both, "tp", scatter_dimension=1, tiled=True).astype(
                jnp.float32
            )
        got = send(projected(x, 1 - part), [(0, 1), (1, 0)], "tp")
        kept = projected(x, part)
        return kept.astype(jnp.float32) + got.astype(jnp.float32)

    for_outer = send(reduced(cross_a).astype(jnp.bfloat16), OUTWARD)
    cross_own = cross(5, [query], [in_3, mid_3], final=True)
    summed = jnp.where(outer, for_outer.astype(jnp.float32), reduced(cross_own))
    mixed = (hidden_in[0].astype(jnp.float32) + summed).astype(jnp.bfloat16)

    attended = self_attention(flags, queries[0], key, value, others, blocks)
    return (attended[None], mixed[None])


def solution(mesh):
    in_specs = (
        P("db", "ctx", "tp"),
        P("db", "ctx", "tp"),
        P("db", "ctx", "tp"),
        P("db", "ctx", "tp"),
        P("db", "ctx", "tp"),
        P("db", "ctx", None),
        P(None, "db", None, "tp"),
        P("tp", "db"),
    )
    out_specs = (P("db", "ctx", "tp"), P("db", "ctx", "tp"))
    return jax.shard_map(shards, mesh=mesh, in_specs=in_specs, out_specs=out_specs, check_vma=False)
```

time: 851 us -> 349 us (0.41)
  the two profiles are of different devices: /device:TPU:1 before, /device:TPU:21 now
where the time goes in v1:
time: 349 us; the launch traced here: 348 us
  Pallas kernels  157 us (45%)
  waiting for transfers between devices  88.9 us (25%)
  starting transfers between devices  66.2 us (19%)
  blocking collectives  19.9 us (6%)
  local copies, waits for them, and re-layouts  9.19 us (3%)
  other arithmetic  5.97 us (2%)
    ppermute x32, waiting for transfers between devices, send(): return lax.ppermute(value, axis, perm)  88.9 us
    pallas_call x6, Pallas kernels, cross_attention(): pl.pallas_call(functools.partial(cross_kernel, base=at, heads=heads, grou...  86.2 us
    ppermute x32, starting transfers between devices, send(): return lax.ppermute(value, axis, perm)  66.2 us
    pallas_call x1, Pallas kernels, self_attention(): pl.pallas_call(functools.partial(self_kernel, group=group, blocks=blocks,...  42.3 us
    pallas_call x4, Pallas kernels, project(): pl.pallas_call(functools.partial(project_kernel, sides=shapes, depth=dept...  28.2 us
    all_gather x1, blocking collectives, shards(): ids = lax.all_gather(neighbours[0].reshape(-1), 'db')  19.9 us
  transfers between devices with their start and end apart: 32, of which 8 were waited for; matrix products, arithmetic and copies ran while one was open for 2% of the time, Pallas kernels for 45%

profile of v1, /device:TPU:21, one launch (start us, length us, event | category | flops | bytes accessed | tf_op | source)
XLA Modules:
  0.0 348.1 jit_solution(10142200356267130822)
XLA Ops:
  3.9 21.0 %collective-permute-done.6.refs_0_ = bf16[256,2048]{1,0:T(8,128)(2,1)S(1)} collective-permute-done((bf16[256,2048]{1,0:T(8,128)(2,1)}, bf16[256,2048]{1,0:T(8,128)(2,1)S(1)}, u32[]{:S(2)}, u32[]{:S(2)}) %collective-permute-start.6) | collective-permute-done | bytes 1048608 | tf_op jit(solution)/shard_map/ppermute | solution.py:348
  34.4 15.7 %collective-permute-done.9.refs_1_ = bf16[256,2048]{1,0:T(8,128)(2,1)} collective-permute-done((bf16[256,2048]{1,0:T(8,128)(2,1)S(1)}, bf16[256,2048]{1,0:T(8,128)(2,1)}, u32[]{:S(2)}, u32[]{:S(2)}) %collective-permute-start.9) | collective-permute-done | bytes 1048608 | tf_op jit(solution)/shard_map/ppermute | solution.py:348
  52.1 3.8 %collective-permute-start.10 = (bf16[256,2048]{1,0:T(8,128)(2,1)}, bf16[256,2048]{1,0:T(8,128)(2,1)}, u32[]{:S(2)}, u32[]{:S(2)}) collective-permute-start(bf16[256,2048]{1,0:T(8,128)(2,1)} %collective-permute-done.9.refs_1_), channel_id=1, source_target_pairs={{2,0},{4,6},{3,1},{5,7},{10,8},{12,14},{11,9},{13,15},{18,16},{20,... | collective-permute-start | bytes 3145736 | tf_op jit(solution)/shard_map/ppermute | solution.py:348
  56.1 19.9 %all-gather = s32[4,1,8]{2,1,0:T(1,128)S(1)} all-gather(s32[1,1,8]{2,1,0:T(1,128)S(1)} %reshape.18), channel_id=1, replica_groups=mesh['ctx'=4,'db'=4,'tp'=2] {'db'}, dimensions={0}, use_global_device_ids=true | all-gather | bytes 160 | tf_op jit(solution)/shard_map/all_gather | solution.py:351
  77.0 4.1 %collective-permute-start.16 = (bf16[512,1024]{1,0:T(8,128)(2,1)S(1)}, bf16[512,1024]{1,0:T(8,128)(2,1)S(1)}, u32[]{:S(2)}, u32[]{:S(2)}) collective-permute-start(bf16[512,1024]{1,0:T(8,128)(2,1)S(1)} %collective-permute-done.13.refs_1_), channel_id=1, source_target_pairs={{0,8},{8,0},{16,24},{24,16},{1,9},{9,1},{17,25},{25,17},{2,10},{10... | collective-permute-start | bytes 3145736 | tf_op jit(solution)/shard_map/ppermute | solution.py:348
  81.1 4.5 %collective-permute-start.22 = (bf16[512,1024]{1,0:T(8,128)(2,1)S(1)}, bf16[512,1024]{1,0:T(8,128)(2,1)S(1)}, u32[]{:S(2)}, u32[]{:S(2)}) collective-permute-start(bf16[512,1024]{1,0:T(8,128)(2,1)S(1)} %collective-permute-done.13.refs_1_), channel_id=1, source_target_pairs={{2,4},{4,2},{3,5},{5,3},{10,12},{12,10},{11,13},{13,11},{18,20},{2... | collective-permute-start | bytes 3145736 | tf_op jit(solution)/shard_map/ppermute | solution.py:348
  92.7 4.7 %collective-permute-done.15.refs_2_ = bf16[512,1024]{1,0:T(8,128)(2,1)S(1)} collective-permute-done((bf16[512,1024]{1,0:T(8,128)(2,1)S(1)}, bf16[512,1024]{1,0:T(8,128)(2,1)S(1)}, u32[]{:S(2)}, u32[]{:S(2)}) %collective-permute-start.15) | collective-permute-done | bytes 1048608 | tf_op jit(solution)/shard_map/ppermute | solution.py:348
  97.7 6.3 %collective-permute-start.17 = (bf16[512,1024]{1,0:T(8,128)(2,1)S(1)}, bf16[512,1024]{1,0:T(8,128)(2,1)S(1)}, u32[]{:S(2)}, u32[]{:S(2)}) collective-permute-start(bf16[512,1024]{1,0:T(8,128)(2,1)S(1)} %collective-permute-done.15.refs_2_), channel_id=1, source_target_pairs={{0,8},{8,0},{16,24},{24,16},{1,9},{9,1},{17,25},{25,17},{2,10},{10... | collective-permute-start | bytes 3145736 | tf_op jit(solution)/shard_map/ppermute | solution.py:348
  104.0 4.9 %collective-permute-done.22.refs_9_ = bf16[512,1024]{1,0:T(8,128)(2,1)S(1)} collective-permute-done((bf16[512,1024]{1,0:T(8,128)(2,1)S(1)}, bf16[512,1024]{1,0:T(8,128)(2,1)S(1)}, u32[]{:S(2)}, u32[]{:S(2)}) %collective-permute-start.22) | collective-permute-done | bytes 1048608 | tf_op jit(solution)/shard_map/ppermute | solution.py:348
  109.7 19.9 %collective-permute-done.11.refs_3_.refs_4_ = bf16[256,2176]{1,0:T(8,128)(2,1)S(1)} collective-permute-done((bf16[256,2176]{1,0:T(8,128)(2,1)S(1)}, bf16[256,2176]{1,0:T(8,128)(2,1)S(1)}, u32[]{:S(2)}, u32[]{:S(2)}) %collective-permute-start.11) | collective-permute-done | bytes 1114144 | tf_op jit(solution)/shard_map/ppermute | solution.py:348
  130.8 21.0 %cross_attention.7 = bf16[256,2176]{1,0:T(8,128)(2,1)} custom-call(s32[78]{0:T(128)S(1)} %reshape.12.meta, bf16[256,2048]{1,0:T(8,128)(2,1)} %collective-permute-done.8.refs_0_, bf16[256,2048]{1,0:T(8,128)(2,1)} %collective-permute-done.9.refs_1_, bf16[2,8,128,2048]{3,2,1,0:T(8,128)(2,1)} %refs_1_.7, ...), custom_call_target="tpu_custom_call" | custom-call | flops 536870912 | bytes 11534336 | tf_op jit(solution)/shard_map/cross_attention/pallas_call | solution.py:222
  154.9 4.8 %collective-permute-start.12 = (bf16[256,2176]{1,0:T(8,128)(2,1)}, bf16[256,2176]{1,0:T(8,128)(2,1)}, u32[]{:S(2)}, u32[]{:S(2)}) collective-permute-start(bf16[256,2176]{1,0:T(8,128)(2,1)} %cross_attention.7), channel_id=1, source_target_pairs={{2,4},{4,2},{3,5},{5,3},{10,12},{12,10},{11,13},{13,11},{18,20},{2... | collective-permute-start | bytes 3342344 | tf_op jit(solution)/shard_map/ppermute | solution.py:348
  161.2 20.1 %collective-permute-done.28.refs_3_.refs_4_ = bf16[256,2176]{1,0:T(8,128)(2,1)S(1)} collective-permute-done((bf16[256,2176]{1,0:T(8,128)(2,1)}, bf16[256,2176]{1,0:T(8,128)(2,1)S(1)}, u32[]{:S(2)}, u32[]{:S(2)}) %collective-permute-start.28) | collective-permute-done | bytes 1114144 | tf_op jit(solution)/shard_map/ppermute | solution.py:348
  182.6 20.9 %cross_attention.10 = bf16[256,2176]{1,0:T(8,128)(2,1)} custom-call(s32[78]{0:T(128)S(1)} %reshape.12.meta, bf16[256,2048]{1,0:T(8,128)(2,1)S(1)} %copy-done.9, bf16[256,2048]{1,0:T(8,128)(2,1)S(1)} %copy-done.13, bf16[2,8,128,2048]{3,2,1,0:T(8,128)(2,1)} %refs_1_.7, bf16[256,2176]{1,0:T(8,128)(2,1)S(1)} %collective-permute-done.28.refs_3_.refs_4_, ...), custom_call_target="tpu_custom_call" | custom-call | flops 536870912 | bytes 11534336 | tf_op jit(solution)/shard_map/cross_attention/pallas_call | solution.py:222
  205.8 4.8 %collective-permute-start.30 = (bf16[256,2176]{1,0:T(8,128)(2,1)}, bf16[256,2176]{1,0:T(8,128)(2,1)}, u32[]{:S(2)}, u32[]{:S(2)}) collective-permute-start(bf16[256,2176]{1,0:T(8,128)(2,1)} %cross_attention.10), channel_id=1, source_target_pairs={{2,4},{4,2},{3,5},{5,3},{10,12},{12,10},{11,13},{13,11},{18,20},{2... | collective-permute-start | bytes 3342344 | tf_op jit(solution)/shard_map/ppermute | solution.py:348
  214.7 19.9 %cross_attention.9.x_ref = bf16[256,2048]{1,0:T(8,128)(2,1)S(1)} custom-call(s32[78]{0:T(128)S(1)} %reshape.12.meta, bf16[256,2048]{1,0:T(8,128)(2,1)S(1)} %copy-done.10, bf16[2,8,128,2048]{3,2,1,0:T(8,128)(2,1)} %refs_1_.7, bf16[256,2176]{1,0:T(8,128)(2,1)} %collective-permute-done.12.refs_2_.refs_3_, ...), custom_call_target="tpu_custom_call" | custom-call | flops 536870912 | bytes 12582912 | tf_op jit(solution)/shard_map/cross_attention/pallas_call | solution.py:222
  234.6 7.5 %project.5 = bf16[256,2048]{1,0:T(8,128)(2,1)} custom-call(s32[8]{0:T(128)S(1)} %stack.144.meta, bf16[256,2048]{1,0:T(8,128)(2,1)S(1)} %cross_attention.9.x_ref, bf16[2048,1024]{1,0:T(8,128)(2,1)} %refs_0_.7, bf16[512,1024]{1,0:T(8,128)(2,1)S(1)} %collective-permute-done.13.refs_1_, bf16[512,1024]{1,0:T(8,128)(2,1)S(1)} %collective-permute-done.15.refs_2_, ...), custom_call_target="tpu_custom_call" | custom-call | flops 2147483648 | bytes 10485760 | tf_op jit(solution)/shard_map/project/pallas_call | solution.py:307
  246.1 6.5 %project.4 = bf16[256,2048]{1,0:T(8,128)(2,1)S(1)} custom-call(s32[8]{0:T(128)S(1)} %stack.131.meta, bf16[256,2048]{1,0:T(8,128)(2,1)S(1)} %copy-done.3, bf16[2048,1024]{1,0:T(8,128)(2,1)} %refs_0_.7, bf16[512,1024]{1,0:T(8,128)(2,1)S(1)} %collective-permute-done.13.refs_1_, bf16[512,1024]{1,0:T(8,128)(2,1)S(1)} %collective-permute-done.15.refs_2_, ...), custom_call_target="tpu_custom_call" | custom-call | flops 2147483648 | bytes 10485760 | tf_op jit(solution)/shard_map/project/pallas_call | solution.py:307
  253.9 5.8 %collective-permute-start.4 = (bf16[256,2048]{1,0:T(8,128)(2,1)}, bf16[256,2048]{1,0:T(8,128)(2,1)}, u32[]{:S(2)}, u32[]{:S(2)}) collective-permute-start(bf16[256,2048]{1,0:T(8,128)(2,1)} %collective-permute-done.2.rest_2_), channel_id=1, source_target_pairs={{16,24},{24,16},{17,25},{25,17},{18,26},{26,18},{19,27},{27,19},{2... | collective-permute-start | bytes 3145736 | tf_op jit(solution)/shard_map/ppermute | solution.py:348
  261.7 20.0 %cross_attention.11.x_ref = bf16[256,2048]{1,0:T(8,128)(2,1)S(1)} custom-call(s32[78]{0:T(128)S(1)} %reshape.12.meta, bf16[256,2048]{1,0:T(8,128)(2,1)S(1)} %bitcast.44, bf16[2,8,128,2048]{3,2,1,0:T(8,128)(2,1)} %refs_1_.7, bf16[256,2176]{1,0:T(8,128)(2,1)} %collective-permute-done.29.refs_2_.refs_3_, ...), custom_call_target="tpu_custom_call" | custom-call | flops 536870912 | bytes 12582912 | tf_op jit(solution)/shard_map/cross_attention/pallas_call | solution.py:222
  281.7 7.5 %project.7 = bf16[256,2048]{1,0:T(8,128)(2,1)} custom-call(s32[8]{0:T(128)S(1)} %stack.144.meta, bf16[256,2048]{1,0:T(8,128)(2,1)S(1)} %cross_attention.11.x_ref, bf16[2048,1024]{1,0:T(8,128)(2,1)} %refs_0_.7, bf16[512,1024]{1,0:T(8,128)(2,1)S(1)} %collective-permute-done.13.refs_1_, bf16[512,1024]{1,0:T(8,128)(2,1)S(1)} %collective-permute-done.15.refs_2_, ...), custom_call_target="tpu_custom_call" | custom-call | flops 2147483648 | bytes 10485760 | tf_op jit(solution)/shard_map/project/pallas_call | solution.py:307
  295.8 42.3 %self_attention.1 = bf16[256,2048]{1,0:T(8,128)(2,1)} custom-call(s32[3]{0:T(128)S(1)} %pad_add_fusion.flags, bf16[256,2048]{1,0:T(8,128)(2,1)S(1)} %bitcast.45, bf16[256,2048]{1,0:T(8,128)(2,1)} %bitcast.3.k_ref, bf16[256,2048]{1,0:T(8,128)(2,1)} %bitcast.4.v_ref, bf16[256,2048]{1,0:T(8,128)(2,1)} %collective-permute-done.rest_0_, ...), custom_call_target="tpu_custom_call" | custom-call | flops 2147483648 | bytes 10485760 | tf_op jit(solution)/shard_map/self_attention/pallas_call | solution.py:83
  338.2 6.6 %project.6 = bf16[256,2048]{1,0:T(8,128)(2,1)S(1)} custom-call(s32[8]{0:T(128)S(1)} %stack.131.meta, bf16[256,2048]{1,0:T(8,128)(2,1)S(1)} %copy-done.1, bf16[2048,1024]{1,0:T(8,128)(2,1)} %refs_0_.7, bf16[512,1024]{1,0:T(8,128)(2,1)S(1)} %collective-permute-done.13.refs_1_, bf16[512,1024]{1,0:T(8,128)(2,1)S(1)} %collective-permute-done.15.refs_2_, ...), custom_call_target="tpu_custom_call" | custom-call | flops 2147483648 | bytes 10485760 | tf_op jit(solution)/shard_map/project/pallas_call | solution.py:307
  344.8 3.3 fusion.1
  (115 shorter events, 51.0 us)
Async XLA Ops:
  33.1 43.5 %collective-permute-start.13 = (bf16[512,1024]{1,0:T(8,128)(2,1)}, bf16[512,1024]{1,0:T(8,128)(2,1)S(1)}, u32[]{:S(2)}, u32[]{:S(2)}) collective-permute-start(bf16[512,1024]{1,0:T(8,128)(2,1)} %constant_dynamic-slice_fusion), channel_id=1, source_target_pairs={{0,2},{6,4},{1,3},{7,5},{8,10},{14,12},{9,11},{15,13},{16,18},{22,... | collective-permute-start | bytes 3145736 | tf_op jit(solution)/shard_map/ppermute | solution.py:348
  50.0 31.0 %collective-permute-start.18 = (bf16[512,1024]{1,0:T(8,128)(2,1)}, bf16[512,1024]{1,0:T(8,128)(2,1)}, u32[]{:S(2)}, u32[]{:S(2)}) collective-permute-start(bf16[512,1024]{1,0:T(8,128)(2,1)} %constant_dynamic-slice_fusion), channel_id=1, source_target_pairs={{2,4},{4,2},{3,5},{5,3},{10,12},{12,10},{11,13},{13,11},{18,20},{2... | collective-permute-start | bytes 3145736 | tf_op jit(solution)/shard_map/ppermute | solution.py:348
  52.1 33.5 %collective-permute-start.10 = (bf16[256,2048]{1,0:T(8,128)(2,1)}, bf16[256,2048]{1,0:T(8,128)(2,1)}, u32[]{:S(2)}, u32[]{:S(2)}) collective-permute-start(bf16[256,2048]{1,0:T(8,128)(2,1)} %collective-permute-done.9.refs_1_), channel_id=1, source_target_pairs={{2,0},{4,6},{3,1},{5,7},{10,8},{12,14},{11,9},{13,15},{18,16},{20,... | collective-permute-start | bytes 3145736 | tf_op jit(solution)/shard_map/ppermute | solution.py:348
  87.8 41.8 %collective-permute-start.11 = (bf16[256,2176]{1,0:T(8,128)(2,1)S(1)}, bf16[256,2176]{1,0:T(8,128)(2,1)S(1)}, u32[]{:S(2)}, u32[]{:S(2)}) collective-permute-start(bf16[256,2176]{1,0:T(8,128)(2,1)S(1)} %cross_attention.6), channel_id=1, source_target_pairs={{0,2},{6,4},{1,3},{7,5},{8,10},{14,12},{9,11},{15,13},{16,18},{22,... | collective-permute-start | bytes 3342344 | tf_op jit(solution)/shard_map/ppermute | solution.py:348
  91.3 62.3 %collective-permute-start.14 = (bf16[256,2176]{1,0:T(8,128)(2,1)S(1)}, bf16[256,2176]{1,0:T(8,128)(2,1)S(1)}, u32[]{:S(2)}, u32[]{:S(2)}) collective-permute-start(bf16[256,2176]{1,0:T(8,128)(2,1)S(1)} %cross_attention.8), channel_id=1, source_target_pairs={{0,2},{6,4},{1,3},{7,5},{8,10},{14,12},{9,11},{15,13},{16,18},{22,... | collective-permute-start | bytes 3342344 | tf_op jit(solution)/shard_map/ppermute | solution.py:348
  97.5 57.4 %collective-permute-start.19 = (bf16[512,1024]{1,0:T(8,128)(2,1)}, bf16[512,1024]{1,0:T(8,128)(2,1)S(1)}, u32[]{:S(2)}, u32[]{:S(2)}) collective-permute-start(bf16[512,1024]{1,0:T(8,128)(2,1)} %collective-permute-done.18.refs_5_), channel_id=1, source_target_pairs={{0,16},{8,24},{16,0},{24,8},{1,17},{9,25},{17,1},{25,9},{2,18},{10... | collective-permute-start | bytes 3145736 | tf_op jit(solution)/shard_map/ppermute | solution.py:348
  97.7 62.0 %collective-permute-start.17 = (bf16[512,1024]{1,0:T(8,128)(2,1)S(1)}, bf16[512,1024]{1,0:T(8,128)(2,1)S(1)}, u32[]{:S(2)}, u32[]{:S(2)}) collective-permute-start(bf16[512,1024]{1,0:T(8,128)(2,1)S(1)} %collective-permute-done.15.refs_2_), channel_id=1, source_target_pairs={{0,8},{8,0},{16,24},{24,16},{1,9},{9,1},{17,25},{25,17},{2,10},{10... | collective-permute-start | bytes 3145736 | tf_op jit(solution)/shard_map/ppermute | solution.py:348
  108.9 51.7 %collective-permute-start.20 = (bf16[512,1024]{1,0:T(8,128)(2,1)}, bf16[512,1024]{1,0:T(8,128)(2,1)S(1)}, u32[]{:S(2)}, u32[]{:S(2)}) collective-permute-start(bf16[512,1024]{1,0:T(8,128)(2,1)} %collective-permute-done.18.refs_5_), channel_id=1, source_target_pairs={{0,8},{8,0},{16,24},{24,16},{1,9},{9,1},{17,25},{25,17},{2,10},{10... | collective-permute-start | bytes 3145736 | tf_op jit(solution)/shard_map/ppermute | solution.py:348
  129.6 31.2 %collective-permute-start.23 = (bf16[512,1024]{1,0:T(8,128)(2,1)S(1)}, bf16[512,1024]{1,0:T(8,128)(2,1)}, u32[]{:S(2)}, u32[]{:S(2)}) collective-permute-start(bf16[512,1024]{1,0:T(8,128)(2,1)S(1)} %collective-permute-done.22.refs_9_), channel_id=1, source_target_pairs={{0,16},{8,24},{16,0},{24,8},{1,17},{9,25},{17,1},{25,9},{2,18},{10... | collective-permute-start | bytes 3145736 | tf_op jit(solution)/shard_map/ppermute | solution.py:348
  154.9 55.7 %collective-permute-start.12 = (bf16[256,2176]{1,0:T(8,128)(2,1)}, bf16[256,2176]{1,0:T(8,128)(2,1)}, u32[]{:S(2)}, u32[]{:S(2)}) collective-permute-start(bf16[256,2176]{1,0:T(8,128)(2,1)} %cross_attention.7), channel_id=1, source_target_pairs={{2,4},{4,2},{3,5},{5,3},{10,12},{12,10},{11,13},{13,11},{18,20},{2... | collective-permute-start | bytes 3342344 | tf_op jit(solution)/shard_map/ppermute | solution.py:348
  159.7 43.8 %collective-permute-start.24 = (bf16[512,1024]{1,0:T(8,128)(2,1)S(1)}, bf16[512,1024]{1,0:T(8,128)(2,1)S(1)}, u32[]{:S(2)}, u32[]{:S(2)}) collective-permute-start(bf16[512,1024]{1,0:T(8,128)(2,1)S(1)} %collective-permute-done.22.refs_9_), channel_id=1, source_target_pairs={{0,8},{8,0},{16,24},{24,16},{1,9},{9,1},{17,25},{25,17},{2,10},{10... | collective-permute-start | bytes 3145736 | tf_op jit(solution)/shard_map/ppermute | solution.py:348
  160.7 44.1 %collective-permute-start.21 = (bf16[512,1024]{1,0:T(8,128)(2,1)S(1)}, bf16[512,1024]{1,0:T(8,128)(2,1)S(1)}, u32[]{:S(2)}, u32[]{:S(2)}) collective-permute-start(bf16[512,1024]{1,0:T(8,128)(2,1)S(1)} %collective-permute-done.19.refs_6_), channel_id=1, source_target_pairs={{0,8},{8,0},{16,24},{24,16},{1,9},{9,1},{17,25},{25,17},{2,10},{10... | collective-permute-start | bytes 3145736 | tf_op jit(solution)/shard_map/ppermute | solution.py:348
  160.8 73.8 %collective-permute-start.25 = (bf16[512,1024]{1,0:T(8,128)(2,1)}, bf16[512,1024]{1,0:T(8,128)(2,1)}, u32[]{:S(2)}, u32[]{:S(2)}) collective-permute-start(bf16[512,1024]{1,0:T(8,128)(2,1)} %collective-permute-done.23.refs_10_), channel_id=1, source_target_pairs={{0,8},{8,0},{16,24},{24,16},{1,9},{9,1},{17,25},{25,17},{2,10},{10... | collective-permute-start | bytes 3145736 | tf_op jit(solution)/shard_map/ppermute | solution.py:348
  181.3 62.2 %collective-permute-start.2 = (bf16[256,2048]{1,0:T(8,128)(2,1)}, bf16[256,2048]{1,0:T(8,128)(2,1)}, u32[]{:S(2)}, u32[]{:S(2)}) collective-permute-start(bf16[256,2048]{1,0:T(8,128)(2,1)} %bitcast.3.k_ref), channel_id=1, source_target_pairs={{0,16},{8,24},{1,17},{9,25},{2,18},{10,26},{3,19},{11,27},{4,20},{... | collective-permute-start | bytes 3145736 | tf_op jit(solution)/shard_map/ppermute | solution.py:348
  203.5 50.4 %collective-permute-start.29 = (bf16[256,2176]{1,0:T(8,128)(2,1)}, bf16[256,2176]{1,0:T(8,128)(2,1)}, u32[]{:S(2)}, u32[]{:S(2)}) collective-permute-start(bf16[256,2176]{1,0:T(8,128)(2,1)} %cross_attention.10), channel_id=1, source_target_pairs={{0,2},{6,4},{1,3},{7,5},{8,10},{14,12},{9,11},{15,13},{16,18},{22,... | collective-permute-start | bytes 3342344 | tf_op jit(solution)/shard_map/ppermute | solution.py:348
  205.8 54.0 %collective-permute-start.30 = (bf16[256,2176]{1,0:T(8,128)(2,1)}, bf16[256,2176]{1,0:T(8,128)(2,1)}, u32[]{:S(2)}, u32[]{:S(2)}) collective-permute-start(bf16[256,2176]{1,0:T(8,128)(2,1)} %cross_attention.10), channel_id=1, source_target_pairs={{2,4},{4,2},{3,5},{5,3},{10,12},{12,10},{11,13},{13,11},{18,20},{2... | collective-permute-start | bytes 3342344 | tf_op jit(solution)/shard_map/ppermute | solution.py:348
  210.6 42.0 %collective-permute-start.3 = (bf16[256,2048]{1,0:T(8,128)(2,1)}, bf16[256,2048]{1,0:T(8,128)(2,1)}, u32[]{:S(2)}, u32[]{:S(2)}) collective-permute-start(bf16[256,2048]{1,0:T(8,128)(2,1)} %bitcast.4.v_ref), channel_id=1, source_target_pairs={{0,16},{8,24},{1,17},{9,25},{2,18},{10,26},{3,19},{11,27},{4,20},{... | collective-permute-start | bytes 3145736 | tf_op jit(solution)/shard_map/ppermute | solution.py:348
  242.2 47.1 %collective-permute-start.26 = (bf16[256,2048]{1,0:T(8,128)(2,1)}, bf16[256,2048]{1,0:T(8,128)(2,1)}, u32[]{:S(2)}, u32[]{:S(2)}) collective-permute-start(bf16[256,2048]{1,0:T(8,128)(2,1)} %project.5), channel_id=1, source_target_pairs={{0,1},{1,0},{2,3},{3,2},{4,5},{5,4},{6,7},{7,6},{8,9},{9,8},{10,11... | collective-permute-start | bytes 3145736 | tf_op jit(solution)/shard_map/ppermute | solution.py:348
  243.4 48.8 %collective-permute-start = (bf16[256,2048]{1,0:T(8,128)(2,1)}, bf16[256,2048]{1,0:T(8,128)(2,1)}, u32[]{:S(2)}, u32[]{:S(2)}) collective-permute-start(bf16[256,2048]{1,0:T(8,128)(2,1)} %bitcast.3.k_ref), channel_id=1, source_target_pairs={{0,8},{16,24},{1,9},{17,25},{2,10},{18,26},{3,11},{19,27},{4,12},{... | collective-permute-start | bytes 3145736 | tf_op jit(solution)/shard_map/ppermute | solution.py:348
  252.6 42.0 %collective-permute-start.1 = (bf16[256,2048]{1,0:T(8,128)(2,1)}, bf16[256,2048]{1,0:T(8,128)(2,1)}, u32[]{:S(2)}, u32[]{:S(2)}) collective-permute-start(bf16[256,2048]{1,0:T(8,128)(2,1)} %bitcast.4.v_ref), channel_id=1, source_target_pairs={{0,8},{16,24},{1,9},{17,25},{2,10},{18,26},{3,11},{19,27},{4,12},{... | collective-permute-start | bytes 3145736 | tf_op jit(solution)/shard_map/ppermute | solution.py:348
  253.9 40.6 %collective-permute-start.4 = (bf16[256,2048]{1,0:T(8,128)(2,1)}, bf16[256,2048]{1,0:T(8,128)(2,1)}, u32[]{:S(2)}, u32[]{:S(2)}) collective-permute-start(bf16[256,2048]{1,0:T(8,128)(2,1)} %collective-permute-done.2.rest_2_), channel_id=1, source_target_pairs={{16,24},{24,16},{17,25},{25,17},{18,26},{26,18},{19,27},{27,19},{2... | collective-permute-start | bytes 3145736 | tf_op jit(solution)/shard_map/ppermute | solution.py:348
  259.8 34.8 %collective-permute-start.5 = (bf16[256,2048]{1,0:T(8,128)(2,1)}, bf16[256,2048]{1,0:T(8,128)(2,1)}, u32[]{:S(2)}, u32[]{:S(2)}) collective-permute-start(bf16[256,2048]{1,0:T(8,128)(2,1)} %collective-permute-done.3.rest_3_), channel_id=1, source_target_pairs={{16,24},{24,16},{17,25},{25,17},{18,26},{26,18},{19,27},{27,19},{2... | collective-permute-start | bytes 3145736 | tf_op jit(solution)/shard_map/ppermute | solution.py:348
  289.3 55.5 %collective-permute-start.31 = (bf16[256,2048]{1,0:T(8,128)(2,1)}, bf16[256,2048]{1,0:T(8,128)(2,1)}, u32[]{:S(2)}, u32[]{:S(2)}) collective-permute-start(bf16[256,2048]{1,0:T(8,128)(2,1)} %project.7), channel_id=1, source_target_pairs={{0,1},{1,0},{2,3},{3,2},{4,5},{5,4},{6,7},{7,6},{8,9},{9,8},{10,11... | collective-permute-start | bytes 3145736 | tf_op jit(solution)/shard_map/ppermute | solution.py:348
  292.2 52.5 %collective-permute-start.27 = (bf16[256,2048]{1,0:T(8,128)(2,1)}, bf16[256,2048]{1,0:T(8,128)(2,1)}, u32[]{:S(2)}, u32[]{:S(2)}) collective-permute-start(bf16[256,2048]{1,0:T(8,128)(2,1)} %add_convert_fusion), channel_id=1, source_target_pairs={{2,0},{4,6},{3,1},{5,7},{10,8},{12,14},{11,9},{13,15},{18,16},{20,... | collective-permute-start | bytes 3145736 | tf_op jit(solution)/shard_map/ppermute | solution.py:348
  (30 other events, 870.0 us)

commit v2 on v1

--- a/solution.py
+++ b/solution.py
@@ -27,6 +27,65 @@
         lax.dot_general(query, key, (((1,), (1,)), ((), ())), preferred_element_type=jnp.float32)
         * SCALE2
     )
+
+
+def with_ones(value):
+    return jnp.concatenate([value, jnp.ones_like(value)], axis=1)
+
+
+def case_kernel(chosen_ref, q_ref, k_ref, v_ref, *rest, group, cases, rows):
+    others, out_ref = rest[:-1], rest[-1]
+    some = [slice(g * DH, (g + 1) * DH) for g in range(group)]
+
+    def run(chosen):
+        row = lax.broadcasted_iota(jnp.int32, (rows, rows), 0)
+        col = lax.broadcasted_iota(jnp.int32, (rows, rows), 1)
+        pairs = [(k_ref, v_ref)] + [(others[2 * i], others[2 * i + 1]) for i in chosen]
+        found = [[scores(q_ref[:, c], key[:, c]) for key, _ in pairs] for c in some]
+        for score in found:
+            score[0] = jnp.where(col <= row, score[0], NEG)
+        peaks = [
+            jnp.max(functools.reduce(jnp.maximum, score), axis=-1, keepdims=True) for score in found
+        ]
+        weights = [
+            [jnp.exp2(part - peak).astype(jnp.bfloat16) for part in score]
+            for score, peak in zip(found, peaks)
+        ]
+        for c, parts in zip(some, weights):
+            both = sum(
+                jnp.dot(part, with_ones(value[:, c]), preferred_element_type=jnp.float32)
+                for part, (_, value) in zip(parts, pairs)
+            )
+            out_ref[:, c] = (both[:, :DH] / both[:, DH:]).astype(jnp.bfloat16)
+
+    for index, chosen in enumerate(cases):
+        pl.when(chosen_ref[0] == index)(functools.partial(run, chosen))
+
+
+def self_attention_cases(chosen, queries, keys, values, others, cases):
+    rows, width = queries.shape
+    heads = width // DH
+    group = math.gcd(heads, 4)
+    spec = pl.BlockSpec((rows, group * DH), lambda h, chosen: (0, h))
+    operands = [queries, keys, values] + [array for pair in others for array in pair]
+    pairs = (len(others) + 1) * rows * rows * heads
+    return pl.pallas_call(
+        functools.partial(case_kernel, group=group, cases=cases, rows=rows),
+        out_shape=jax.ShapeDtypeStruct((rows, width), jnp.bfloat16),
+        grid_spec=pltpu.PrefetchScalarGridSpec(
+            num_scalar_prefetch=1,
+            grid=(heads // group,),
+            in_specs=[spec] * len(operands),
+            out_specs=spec,
+        ),
+        compiler_params=pltpu.CompilerParams(vmem_limit_bytes=VMEM_BYTES),
+        cost_estimate=pl.CostEstimate(
+            flops=4 * pairs * DH,
+            bytes_accessed=(len(operands) + 1) * rows * width * 2,
+            transcendentals=pairs,
+        ),
+        name="self_attention",
+    )(chosen, *operands)
 
 
 def self_kernel(flags, q_ref, k_ref, v_ref, *rest, group, blocks, rows):
@@ -108,123 +167,151 @@
     refs = list(refs)
     query_refs = [refs.pop(0) for _ in range(1 + two_queries)]
     database_ref = refs.pop(0)
-    state_refs = [(refs.pop(0), refs.pop(0)) for _ in range(states)]
-    out_ref = refs.pop(0)
-    step = pl.program_id(0)
+    state_refs = [refs.pop(0) for _ in range(states)]
+    out_ref, query, came, held, peak_ref, total_ref, accum_ref, sems, more = refs
     width = heads * DH
-    length = database_ref.shape[2]
+    rows = span_count * SPAN
+    entries = span_count * near
+    used = [meta[base + 3 + i] == 1 for i in range(states)]
+    every = [slice(h * DH, (h + 1) * DH) for h in range(heads)]
+
+    def fetch(entry, index):
+        place = jnp.maximum(meta[base + 5 + entry], 0)
+        return pltpu.make_async_copy(
+            database_ref.at[index, place], held.at[index, entry], sems.at[index, entry]
+        )
 
     @pl.when(meta[base] == 1)
     def _():
-        lane = lax.broadcasted_iota(jnp.int32, (SPAN, LANES), 1)
-        for u in range(span_count):
-            rows = slice(u * SPAN, (u + 1) * SPAN)
-            places = [meta[base + 5 + u * near + n] for n in range(near)]
-            stats = [
-                jnp.where(meta[base + 3 + i] == 1, 1.0, 0.0) * ref[rows, :].astype(jnp.float32)
-                for i, (_, ref) in enumerate(state_refs)
-            ]
-            coded = jnp.zeros((SPAN, LANES), jnp.float32)
-            for g in range(group):
-                cols = slice(g * DH, (g + 1) * DH)
-                head = step * group + g
-                mine = (lane == head) | (lane == heads + head) | (lane == 2 * heads + head)
-                query = query_refs[0][rows, cols]
-                if two_queries:
-                    query = jnp.where(meta[base + 1] == 1, query, query_refs[1][rows, cols])
-                found = []
-                for place in places:
-                    key = database_ref[0, jnp.maximum(place, 0), :, cols]
-                    found.append(jnp.where(place >= 0, scores(query, key), NEG))
-                came = []
-                for i in range(states):
-                    level = jnp.sum(jnp.where(mine, stats[i], 0.0), axis=-1, keepdims=True)
-                    came.append(jnp.where(meta[base + 3 + i] == 1, level, NEG))
-                peak = jnp.full((SPAN, 1), FLOOR, jnp.float32)
-                for score in found:
-                    peak = jnp.maximum(peak, jnp.max(score, axis=-1, keepdims=True))
-                for level in came:
+        gets = [
+            pltpu.make_async_copy(ref, came.at[i], more.at[1 + i])
+            for i, ref in enumerate(state_refs)
+        ]
+        for i, get in enumerate(gets):
+            pl.when(used[i])(get.start)
+        picks = [pltpu.make_async_copy(ref, query, more.at[0]) for ref in query_refs]
+        if two_queries:
+            pl.when(meta[base + 1] == 1)(picks[0].start)
+            pl.when(meta[base + 1] == 0)(picks[1].start)
+        else:
+            picks[0].start()
+        for entry in range(entries):
+
+            @pl.when(meta[base + 5 + entry] >= 0)
+            def _(entry=entry):
+                fetch(entry, 0).start()
+                fetch(entry, 1).start()
+
+        lane = lax.broadcasted_iota(jnp.int32, (1, LANES), 1)
+        line = lax.broadcasted_iota(jnp.int32, (LANES, LANES), 0)
+        for i, get in enumerate(gets):
+            pl.when(used[i])(get.wait)
+        if states:
+            stats = [came[i, :, width:] for i in range(states)]
+            for h, cols in enumerate(every):
+                spread = (line == h) | (line == heads + h) | (line == 2 * heads + h)
+                levels = [
+                    jnp.where(
+                        used[i],
+                        jnp.dot(
+                            stats[i],
+                            spread.astype(jnp.bfloat16),
+                            preferred_element_type=jnp.float32,
+                        ),
+                        NEG,
+                    )
+                    for i in range(states)
+                ]
+                peak = jnp.full((rows, LANES), FLOOR, jnp.float32)
+                for level in levels:
                     peak = jnp.maximum(peak, level)
-                total = jnp.zeros((SPAN, 1), jnp.float32)
-                accum = jnp.zeros((SPAN, DH), jnp.float32)
-                for place, score in zip(places, found):
-                    weights = jnp.exp2(score - peak)
-                    total += jnp.sum(weights, axis=-1, keepdims=True)
-                    accum += jnp.dot(
-                        weights.astype(jnp.bfloat16),
-                        database_ref[1, jnp.maximum(place, 0), :, cols],
-                        preferred_element_type=jnp.float32,
-                    )
-                for i, level in enumerate(came):
-                    factor = jnp.exp2(level - peak)
-                    total += factor
-                    accum += factor * jnp.where(
-                        meta[base + 3 + i] == 1,
-                        state_refs[i][0][rows, cols].astype(jnp.float32),
-                        0.0,
-                    )
-                some = total > 0.0
-                safe = jnp.where(some, total, 1.0)
-                result = (accum / safe).astype(jnp.bfloat16)
-                if final:
-                    out_ref[rows, cols] = result
-                    continue
-                at = pl.multiple_of(step * (group * DH) + g * DH, DH)
-                out_ref[rows, pl.ds(at, DH)] = result
-                level = jnp.where(some, peak + jnp.log2(safe), NEG)
-                high = level.astype(jnp.bfloat16).astype(jnp.float32)
-                mid = (level - high).astype(jnp.bfloat16).astype(jnp.float32)
-                low = level - high - mid
-                coded += jnp.where(
-                    lane == head,
-                    high,
-                    jnp.where(
-                        lane == heads + head, mid, jnp.where(lane == 2 * heads + head, low, 0.0)
-                    ),
+                factors = [jnp.exp2(level - peak) for level in levels]
+                peak_ref[:, cols] = peak
+                total_ref[:, cols] = sum(factors)
+                accum_ref[:, cols] = sum(
+                    jnp.where(used[i], factor * came[i, :, cols].astype(jnp.float32), 0.0)
+                    for i, factor in enumerate(factors)
                 )
+        else:
+            peak_ref[...] = jnp.full((rows, width), FLOOR, jnp.float32)
+            total_ref[...] = jnp.zeros((rows, width), jnp.float32)
+            accum_ref[...] = jnp.zeros((rows, width), jnp.float32)
+        picks[0].wait()
+
+        @pl.loop(0, entries)
+        def _(entry):
+            @pl.when(meta[base + 5 + entry] >= 0)
+            def _():
+                fetch(entry, 0).wait()
+                fetch(entry, 1).wait()
+                here = pl.ds(pl.multiple_of((entry // near) * SPAN, SPAN), SPAN)
+                for start in range(0, heads, group):
+                    some = every[start : start + group]
+                    found = [scores(query[here, c], held[0, entry, :, c]) for c in some]
+                    before = [peak_ref[here, c] for c in some]
+                    peaks = [
+                        jnp.maximum(old, jnp.max(score, axis=-1, keepdims=True))
+                        for old, score in zip(before, found)
+                    ]
+                    weights = [
+                        jnp.exp2(score - peak).astype(jnp.bfloat16)
+                        for score, peak in zip(found, peaks)
+                    ]
+                    factors = [jnp.exp2(old - peak) for old, peak in zip(before, peaks)]
+                    both = [
+                        jnp.dot(
+                            weight,
+                            with_ones(held[1, entry, :, c]),
+                            preferred_element_type=jnp.float32,
+                        )
+                        for weight, c in zip(weights, some)
+                    ]
+                    accums = [
+                        accum_ref[here, c] * factor + pair[:, :DH]
+                        for c, factor, pair in zip(some, factors, both)
+                    ]
+                    totals = [
+                        total_ref[here, c] * factor + pair[:, DH:]
+                        for c, factor, pair in zip(some, factors, both)
+                    ]
+                    for c, peak, accum, total in zip(some, peaks, accums, totals):
+                        peak_ref[here, c] = peak
+                        accum_ref[here, c] = accum
+                        total_ref[here, c] = total
+
+        packed = jnp.zeros((rows, LANES), jnp.float32)
+        for h, cols in enumerate(every):
+            total = total_ref[:, cols]
+            safe = jnp.where(total > 0.0, total, 1.0)
+            out_ref[:, cols] = (accum_ref[:, cols] / safe).astype(jnp.bfloat16)
             if not final:
-                before = jnp.where(step == 0, 0.0, 1.0) * jnp.where(
-                    step == 0, 0.0, out_ref[rows, width:].astype(jnp.float32)
-                )
-                out_ref[rows, width:] = (before + coded).astype(jnp.bfloat16)
+                level = jnp.where(total > 0.0, peak_ref[:, cols] + jnp.log2(safe), NEG)
+                packed = jnp.where(lane == h, level, packed)
+        if not final:
+            high = packed.astype(jnp.bfloat16).astype(jnp.float32)
+            mid = (packed - high).astype(jnp.bfloat16).astype(jnp.float32)
+            low = packed - high - mid
+            coded = high + pltpu.roll(mid, heads, 1) + pltpu.roll(low, 2 * heads, 1)
+            out_ref[:, width:] = coded.astype(jnp.bfloat16)
 
 
 def cross_attention(meta, base, queries, database, states, final):
     rows, width = queries[0].shape
     heads = width // DH
-    group = math.gcd(heads, 4)
-    wide = group * DH
-    near = (meta.shape[1] - 5) // (rows // SPAN)
+    assert 3 * heads <= LANES
     span_count = rows // SPAN
-    at = base * meta.shape[1]
-    per_owner, length = database.shape[1], database.shape[2]
-    in_specs = [
-        pl.BlockSpec((rows, wide), lambda h, meta, i=i: (0, h * meta[at + 1 + i]))
-        for i in range(len(queries))
-    ]
-    in_specs.append(
-        pl.BlockSpec(
-            (2, per_owner, length, wide), lambda h, meta: (0, 0, 0, h * meta[at])
-        )
-    )
-    operands = [*queries, database]
-    for i, state in enumerate(states):
-        in_specs.append(pl.BlockSpec((rows, wide), lambda h, meta, i=i: (0, h * meta[at + 3 + i])))
-        in_specs.append(pl.BlockSpec((rows, LANES), lambda h, meta: (0, heads)))
-        operands += [state, state]
-    if final:
-        out_width = width
-        out_spec = pl.BlockSpec((rows, wide), lambda h, meta: (0, h))
-    else:
-        out_width = width + LANES
-        out_spec = pl.BlockSpec((rows, out_width), lambda h, meta: (0, 0))
-    pairs = rows * near * length * heads
+    near = (meta.shape[1] - 5) // span_count
+    entries = span_count * near
+    length = database.shape[2]
+    out_width = width if final else width + LANES
+    anywhere = pl.BlockSpec(memory_space=pl.ANY)
+    pairs = rows * near * length * heads // 4
     return pl.pallas_call(
         functools.partial(
             cross_kernel,
-            base=at,
+            base=base * meta.shape[1],
             heads=heads,
-            group=group,
+            group=heads,
             span_count=span_count,
             near=near,
             two_queries=len(queries) - 1,
@@ -232,20 +319,27 @@
             final=final,
         ),
         out_shape=jax.ShapeDtypeStruct((rows, out_width), jnp.bfloat16),
-        grid_spec=pltpu.PrefetchScalarGridSpec(
-            num_scalar_prefetch=1,
-            grid=(heads // group,),
-            in_specs=in_specs,
-            out_specs=out_spec,
-        ),
+        in_specs=[pl.BlockSpec(memory_space=pltpu.SMEM)]
+        + [anywhere] * (len(queries) + 1 + len(states)),
+        out_specs=pl.BlockSpec(memory_space=pltpu.VMEM),
+        scratch_shapes=[
+            pltpu.VMEM((rows, width), jnp.bfloat16),
+            pltpu.VMEM((max(len(states), 1), rows, width + LANES), jnp.bfloat16),
+            pltpu.VMEM((2, entries, length, width), jnp.bfloat16),
+            pltpu.VMEM((rows, width), jnp.float32),
+            pltpu.VMEM((rows, width), jnp.float32),
+            pltpu.VMEM((rows, width), jnp.float32),
+            pltpu.SemaphoreType.DMA((2, entries)),
+            pltpu.SemaphoreType.DMA((3,)),
+        ],
         compiler_params=pltpu.CompilerParams(vmem_limit_bytes=VMEM_BYTES),
         cost_estimate=pl.CostEstimate(
             flops=4 * pairs * DH,
-            bytes_accessed=database.size * 2 + rows * width * 2 * (2 + len(states)),
+            bytes_accessed=database.size // 2 + rows * width * 2 * (2 + len(states)),
             transcendentals=pairs,
         ),
         name="cross_attention",
-    )(meta.reshape(-1), *operands)
+    )(meta.reshape(-1), *queries, database, *states)
 
 
 def project_kernel(meta, x_ref, *refs, sides, depth, columns, tile):
@@ -348,9 +442,12 @@
         return lax.ppermute(value, axis, perm)
 
     query = cross_queries[0]
-    ids = lax.all_gather(neighbours[0].reshape(-1), "db")
     query_a = send(query, PAIR)
     query_m = send(query, MIDDLE)
+    own_ids = neighbours[0].reshape(-1)
+    ids = [own_ids] + [
+        send(own_ids, [(i, (i + step) % 4) for i in range(4)]) for step in range(1, 4)
+    ]
 
     key, value = keys[0], values[0]
     if two_level:
@@ -360,9 +457,14 @@
         value_c = send(value, [(0, 1), (2, 3)], "ctx")
         key_yc = send(key_y, [(2, 3), (3, 2)], "ctx")
         value_yc = send(value_y, [(2, 3), (3, 2)], "ctx")
-        flags = jnp.stack([member % 2, member // 2, member // 2]).astype(jnp.int32)
-        others = [(key_c, value_c), (key_y, value_y), (key_yc, value_yc)]
-        blocks = [(0, 0), (1, 0), (2, 0)]
+        attended = self_attention_cases(
+            member.astype(jnp.int32)[None],
+            queries[0],
+            key,
+            value,
+            [(key_c, value_c), (key_y, value_y), (key_yc, value_yc)],
+            [[], [0], [1, 2], [0, 1, 2]],
+        )
     else:
         others = [
             (
@@ -372,6 +474,7 @@
         ]
         blocks = [(0, j * rows) for j in range(member_count)]
         flags = (jnp.arange(member_count) < member).astype(jnp.int32)
+        attended = self_attention(flags, queries[0], key, value, others, blocks)
 
     depth = out_weight.shape[0]
     share = depth // member_count
@@ -381,7 +484,8 @@
     share_a = send(after(own_share, query_a), INWARD)
     share_b = send(after(own_share, query_c), MIDDLE)
     share_c = send(after(share_a, share_b), MIDDLE)
-    query_c_out = send(after(query_c, query_b_out), OUTWARD)
+    waited = (key_y, value_y) if two_level else ()
+    query_c_out = send(after(query_c, query_b_out, *waited), OUTWARD)
 
     def whole(piece):
         if not two_level:
@@ -392,6 +496,7 @@
         return [(piece, (4,)), (across, (5,)), (beside, (6,)), (corner, (7,))]
 
     per_owner = database.shape[1]
+    ids = jnp.stack(ids)
     local = jnp.where(ids // per_owner == plane, ids % per_owner, -1)
     seq_a = plane ^ 1
     seq_b = jnp.where(plane < 2, 2, 1)
@@ -403,7 +508,7 @@
 
     def described(active, first, second, state, other, seq):
         head = jnp.stack([active, first, second, state, other]).astype(jnp.int32)
-        return jnp.concatenate([head, lax.dynamic_index_in_dim(local, seq, 0, keepdims=False)])
+        return jnp.concatenate([head, lax.dynamic_index_in_dim(local, (plane - seq) % 4, 0, keepdims=False)])
 
     meta = jnp.stack(
         [
@@ -422,7 +527,7 @@
     own_part = send(after(cross(0, [query]), share_a), INWARD)
     in_1 = send(cross(1, [query_c_out]), INWARD)
     pieces_a, pieces_b, pieces_c = whole(share_a), whole(share_b), whole(share_c)
-    part_2 = cross(2, [query_b_out, query_c], [in_1])
+    part_2 = cross(2, [query_b_out, after(query_c, attended)], [in_1])
     in_2 = send(part_2, INWARD)
     mid_2 = send(part_2, MIDDLE)
     part_3 = cross(3, [query_a, query_m], [in_2])
@@ -455,7 +560,6 @@
     summed = jnp.where(outer, for_outer.astype(jnp.float32), reduced(cross_own))
     mixed = (hidden_in[0].astype(jnp.float32) + summed).astype(jnp.bfloat16)
 
-    attended = self_attention(flags, queries[0], key, value, others, blocks)
     return (attended[None], mixed[None])
 
 

time: 349 us -> 266 us (0.76)
  the two profiles are of different devices: /device:TPU:21 before, /device:TPU:1 now
where the time goes in v2:
time: 266 us; the launch traced here: 265 us
  waiting for transfers between devices  147 us (55%)
  starting transfers between devices  70.2 us (26%)
  Pallas kernels  29.8 us (11%)
  local copies, waits for them, and re-layouts  13.7 us (5%)
  other arithmetic  3.38 us (1%)
    ppermute x35, waiting for transfers between devices, send(): return lax.ppermute(value, axis, perm)  147 us
    ppermute x35, starting transfers between devices, send(): return lax.ppermute(value, axis, perm)  70.2 us
    pallas_call x6, Pallas kernels, cross_attention(): pl.pallas_call(functools.partial(cross_kernel, base=base * meta.shape[1],...  19.5 us
    unnamed x55, local copies, waits for them, and re-layouts  10.4 us
    pallas_call x1, Pallas kernels, self_attention_cases(): pl.pallas_call(functools.partial(case_kernel, group=group, cases=cases, r...  6.61 us
  transfers between devices with their start and end apart: 35, of which 12 were waited for; matrix products, arithmetic and copies ran while one was open for 2% of the time, Pallas kernels for 11%

profile of v2, /device:TPU:1, one launch (start us, length us, event | category | flops | bytes accessed | tf_op | source)
XLA Modules:
  0.0 264.9 jit_solution(2752670535582727091)
XLA Ops:
  0.7 2.2 collective-permute-start.9
  3.6 3.2 %collective-permute-start.2 = (bf16[256,2048]{1,0:T(8,128)(2,1)}, bf16[256,2048]{1,0:T(8,128)(2,1)S(1)}, u32[]{:S(2)}, u32[]{:S(2)}) collective-permute-start(bf16[256,2048]{1,0:T(8,128)(2,1)} %bitcast.47), channel_id=1, source_target_pairs={{0,16},{8,24},{1,17},{9,25},{2,18},{10,26},{3,19},{11,27},{4,20},{... | collective-permute-start | bytes 3145736 | tf_op jit(solution)/shard_map/ppermute | solution.py:442
  8.2 17.8 %collective-permute-done.9.refs_0_ = bf16[256,2048]{1,0:T(8,128)(2,1)S(1)} collective-permute-done((bf16[256,2048]{1,0:T(8,128)(2,1)}, bf16[256,2048]{1,0:T(8,128)(2,1)S(1)}, u32[]{:S(2)}, u32[]{:S(2)}) %collective-permute-start.9) | collective-permute-done | bytes 1048608 | tf_op jit(solution)/shard_map/ppermute | solution.py:442
  31.3 19.7 %collective-permute-done.3.rest_3_ = bf16[256,2048]{1,0:T(8,128)(2,1)S(1)} collective-permute-done((bf16[256,2048]{1,0:T(8,128)(2,1)}, bf16[256,2048]{1,0:T(8,128)(2,1)S(1)}, u32[]{:S(2)}, u32[]{:S(2)}) %collective-permute-start.3) | collective-permute-done | bytes 1048608 | tf_op jit(solution)/shard_map/ppermute | solution.py:442
  51.0 3.2 %collective-permute-done.11.refs_0_ = bf16[256,2048]{1,0:T(8,128)(2,1)S(1)} collective-permute-done((bf16[256,2048]{1,0:T(8,128)(2,1)S(1)}, bf16[256,2048]{1,0:T(8,128)(2,1)S(1)}, u32[]{:S(2)}, u32[]{:S(2)}) %collective-permute-start.11) | collective-permute-done | bytes 1048608 | tf_op jit(solution)/shard_map/ppermute | solution.py:442
  56.5 2.3 constant_dynamic-slice_fusion
  58.8 5.0 %collective-permute-start.16 = (bf16[512,1024]{1,0:T(8,128)(2,1)}, bf16[512,1024]{1,0:T(8,128)(2,1)S(1)}, u32[]{:S(2)}, u32[]{:S(2)}) collective-permute-start(bf16[512,1024]{1,0:T(8,128)(2,1)} %constant_dynamic-slice_fusion), channel_id=1, source_target_pairs={{0,2},{6,4},{1,3},{7,5},{8,10},{14,12},{9,11},{15,13},{16,18},{22,... | collective-permute-start | bytes 3145736 | tf_op jit(solution)/shard_map/ppermute | solution.py:442
  66.0 19.7 %collective-permute-done.6 = s32[8]{0:T(128)S(1)} collective-permute-done((s32[8]{0:T(128)S(1)}, s32[8]{0:T(128)S(1)}, u32[]{:S(2)}, u32[]{:S(2)}) %collective-permute-start.6) | collective-permute-done | bytes 64 | tf_op jit(solution)/shard_map/ppermute | solution.py:442
  89.1 2.4 collective-permute-done.8
  96.9 6.0 %cross_attention.6 = bf16[256,2176]{1,0:T(8,128)(2,1)S(1)} custom-call(s32[78]{0:T(128)S(1)} %reshape.12.meta, bf16[256,2048]{1,0:T(8,128)(2,1)} %collective-permute-done.13.refs_0_, bf16[2,8,128,2048]{3,2,1,0:T(8,128)(2,1)} %refs_1_.7), custom_call_target="tpu_custom_call" | custom-call | flops 134217728 | bytes 4194304 | tf_op jit(solution)/shard_map/cross_attention/pallas_call | solution.py:309
  104.6 10.2 %collective-permute-start.18 = (bf16[512,1024]{1,0:T(8,128)(2,1)S(1)}, bf16[512,1024]{1,0:T(8,128)(2,1)S(1)}, u32[]{:S(2)}, u32[]{:S(2)}) collective-permute-start(bf16[512,1024]{1,0:T(8,128)(2,1)S(1)} %collective-permute-done.16.refs_1_), channel_id=1, source_target_pairs={{0,16},{8,24},{16,0},{24,8},{1,17},{9,25},{17,1},{25,9},{2,18},{10... | collective-permute-start | bytes 3145736 | tf_op jit(solution)/shard_map/ppermute | solution.py:442
  116.5 3.6 %cross_attention.8 = bf16[256,2176]{1,0:T(8,128)(2,1)S(1)} custom-call(s32[78]{0:T(128)S(1)} %reshape.12.meta, bf16[256,2048]{1,0:T(8,128)(2,1)S(1)} %bitcast.44, bf16[2,8,128,2048]{3,2,1,0:T(8,128)(2,1)} %refs_1_.7), custom_call_target="tpu_custom_call" | custom-call | flops 134217728 | bytes 4194304 | tf_op jit(solution)/shard_map/cross_attention/pallas_call | solution.py:309
  121.5 6.6 %self_attention.1 = bf16[256,2048]{1,0:T(8,128)(2,1)} custom-call(s32[1]{0:T(128)} %bitcast.chosen_ref, bf16[256,2048]{1,0:T(8,128)(2,1)S(1)} %bitcast.46, bf16[256,2048]{1,0:T(8,128)(2,1)S(1)} %bitcast.49, bf16[256,2048]{1,0:T(8,128)(2,1)S(1)} %bitcast.52, bf16[256,2048]{1,0:T(8,128)(2,1)} %collective-permute-done.rest_0_, ...), custom_call_target="tpu_custom_call" | custom-call | flops 2147483648 | bytes 10485760 | tf_op jit(solution)/shard_map/self_attention/pallas_call | solution.py:72
  128.1 10.9 %collective-permute-start.22 = (bf16[512,1024]{1,0:T(8,128)(2,1)}, bf16[512,1024]{1,0:T(8,128)(2,1)}, u32[]{:S(2)}, u32[]{:S(2)}) collective-permute-start(bf16[512,1024]{1,0:T(8,128)(2,1)} %collective-permute-done.21.refs_5_), channel_id=1, source_target_pairs={{0,16},{8,24},{16,0},{24,8},{1,17},{9,25},{17,1},{25,9},{2,18},{10... | collective-permute-start | bytes 3145736 | tf_op jit(solution)/shard_map/ppermute | solution.py:442
  140.3 3.8 %cross_attention.7 = bf16[256,2176]{1,0:T(8,128)(2,1)S(1)} custom-call(s32[78]{0:T(128)S(1)} %reshape.12.meta, bf16[256,2048]{1,0:T(8,128)(2,1)S(1)} %copy-done.16, bf16[256,2048]{1,0:T(8,128)(2,1)S(1)} %copy-done.14, bf16[2,8,128,2048]{3,2,1,0:T(8,128)(2,1)} %refs_1_.7, bf16[256,2176]{1,0:T(8,128)(2,1)S(1)} %collective-permute-done.14.refs_3_), custom_call_target="tpu_custom_call" | custom-call | flops 134217728 | bytes 5242880 | tf_op jit(solution)/shard_map/cross_attention/pallas_call | solution.py:309
  144.1 4.3 %collective-permute-start.31 = (bf16[256,2176]{1,0:T(8,128)(2,1)S(1)}, bf16[256,2176]{1,0:T(8,128)(2,1)S(1)}, u32[]{:S(2)}, u32[]{:S(2)}) collective-permute-start(bf16[256,2176]{1,0:T(8,128)(2,1)S(1)} %cross_attention.7), channel_id=1, source_target_pairs={{0,2},{6,4},{1,3},{7,5},{8,10},{14,12},{9,11},{15,13},{16,18},{22,... | collective-permute-start | bytes 3342344 | tf_op jit(solution)/shard_map/ppermute | solution.py:442
  150.1 13.0 %collective-permute-done.22.refs_6_ = bf16[512,1024]{1,0:T(8,128)(2,1)} collective-permute-done((bf16[512,1024]{1,0:T(8,128)(2,1)}, bf16[512,1024]{1,0:T(8,128)(2,1)}, u32[]{:S(2)}, u32[]{:S(2)}) %collective-permute-start.22) | collective-permute-done | bytes 1048608 | tf_op jit(solution)/shard_map/ppermute | solution.py:442
  163.6 20.8 %collective-permute-done.26.refs_10_ = bf16[512,1024]{1,0:T(8,128)(2,1)} collective-permute-done((bf16[512,1024]{1,0:T(8,128)(2,1)}, bf16[512,1024]{1,0:T(8,128)(2,1)}, u32[]{:S(2)}, u32[]{:S(2)}) %collective-permute-start.26) | collective-permute-done | bytes 1048608 | tf_op jit(solution)/shard_map/ppermute | solution.py:442
  184.9 4.7 %cross_attention.10 = bf16[256,2176]{1,0:T(8,128)(2,1)} custom-call(s32[78]{0:T(128)S(1)} %reshape.12.meta, bf16[256,2048]{1,0:T(8,128)(2,1)S(1)} %copy-done.3, bf16[256,2048]{1,0:T(8,128)(2,1)S(1)} %copy-done.12, bf16[2,8,128,2048]{3,2,1,0:T(8,128)(2,1)} %refs_1_.7, bf16[256,2176]{1,0:T(8,128)(2,1)S(1)} %collective-permute-done.31.refs_3_), custom_call_target="tpu_custom_call" | custom-call | flops 134217728 | bytes 5242880 | tf_op jit(solution)/shard_map/cross_attention/pallas_call | solution.py:309
  189.6 6.0 %collective-permute-start.32 = (bf16[256,2176]{1,0:T(8,128)(2,1)}, bf16[256,2176]{1,0:T(8,128)(2,1)}, u32[]{:S(2)}, u32[]{:S(2)}) collective-permute-start(bf16[256,2176]{1,0:T(8,128)(2,1)} %cross_attention.10), channel_id=1, source_target_pairs={{0,2},{6,4},{1,3},{7,5},{8,10},{14,12},{9,11},{15,13},{16,18},{22,... | collective-permute-start | bytes 3342344 | tf_op jit(solution)/shard_map/ppermute | solution.py:442
  207.8 11.2 %collective-permute-done.32.refs_2_ = bf16[256,2176]{1,0:T(8,128)(2,1)} collective-permute-done((bf16[256,2176]{1,0:T(8,128)(2,1)}, bf16[256,2176]{1,0:T(8,128)(2,1)}, u32[]{:S(2)}, u32[]{:S(2)}) %collective-permute-start.32) | collective-permute-done | bytes 1114144 | tf_op jit(solution)/shard_map/ppermute | solution.py:442
  221.9 8.2 %collective-permute-done.29 = bf16[256,2048]{1,0:T(8,128)(2,1)} collective-permute-done((bf16[256,2048]{1,0:T(8,128)(2,1)}, bf16[256,2048]{1,0:T(8,128)(2,1)}, u32[]{:S(2)}, u32[]{:S(2)}) %collective-permute-start.29) | collective-permute-done | bytes 1048608 | tf_op jit(solution)/shard_map/ppermute | solution.py:442
  233.8 18.7 %collective-permute-done.34 = bf16[256,2048]{1,0:T(8,128)(2,1)S(1)} collective-permute-done((bf16[256,2048]{1,0:T(8,128)(2,1)S(1)}, bf16[256,2048]{1,0:T(8,128)(2,1)S(1)}, u32[]{:S(2)}, u32[]{:S(2)}) %collective-permute-start.34) | collective-permute-done | bytes 1048608 | tf_op jit(solution)/shard_map/ppermute | solution.py:442
  252.5 10.7 %collective-permute-done.30 = bf16[256,2048]{1,0:T(8,128)(2,1)S(1)} collective-permute-done((bf16[256,2048]{1,0:T(8,128)(2,1)S(1)}, bf16[256,2048]{1,0:T(8,128)(2,1)S(1)}, u32[]{:S(2)}, u32[]{:S(2)}) %collective-permute-start.30) | collective-permute-done | bytes 1048608 | tf_op jit(solution)/shard_map/ppermute | solution.py:442
  (130 shorter events, 49.6 us)
Async XLA Ops:
  0.7 25.3 %collective-permute-start.9 = (bf16[256,2048]{1,0:T(8,128)(2,1)}, bf16[256,2048]{1,0:T(8,128)(2,1)S(1)}, u32[]{:S(2)}, u32[]{:S(2)}) collective-permute-start(bf16[256,2048]{1,0:T(8,128)(2,1)} %bitcast.42), channel_id=1, source_target_pairs={{0,2},{2,0},{4,6},{6,4},{1,3},{3,1},{5,7},{7,5},{8,10},{10,8},{12,... | collective-permute-start | bytes 3145736 | tf_op jit(solution)/shard_map/ppermute | solution.py:442
  3.6 27.7 %collective-permute-start.2 = (bf16[256,2048]{1,0:T(8,128)(2,1)}, bf16[256,2048]{1,0:T(8,128)(2,1)S(1)}, u32[]{:S(2)}, u32[]{:S(2)}) collective-permute-start(bf16[256,2048]{1,0:T(8,128)(2,1)} %bitcast.47), channel_id=1, source_target_pairs={{0,16},{8,24},{1,17},{9,25},{2,18},{10,26},{3,19},{11,27},{4,20},{... | collective-permute-start | bytes 3145736 | tf_op jit(solution)/shard_map/ppermute | solution.py:442
  6.8 44.2 %collective-permute-start.3 = (bf16[256,2048]{1,0:T(8,128)(2,1)}, bf16[256,2048]{1,0:T(8,128)(2,1)S(1)}, u32[]{:S(2)}, u32[]{:S(2)}) collective-permute-start(bf16[256,2048]{1,0:T(8,128)(2,1)} %bitcast.50), channel_id=1, source_target_pairs={{0,16},{8,24},{1,17},{9,25},{2,18},{10,26},{3,19},{11,27},{4,20},{... | collective-permute-start | bytes 3145736 | tf_op jit(solution)/shard_map/ppermute | solution.py:442
  27.7 26.5 %collective-permute-start.11 = (bf16[256,2048]{1,0:T(8,128)(2,1)S(1)}, bf16[256,2048]{1,0:T(8,128)(2,1)S(1)}, u32[]{:S(2)}, u32[]{:S(2)}) collective-permute-start(bf16[256,2048]{1,0:T(8,128)(2,1)S(1)} %collective-permute-done.10.refs_1_), channel_id=1, source_target_pairs={{2,0},{4,6},{3,1},{5,7},{10,8},{12,14},{11,9},{13,15},{18,16},{20,... | collective-permute-start | bytes 3145736 | tf_op jit(solution)/shard_map/ppermute | solution.py:442
  30.0 62.8 %collective-permute-start = (bf16[256,2048]{1,0:T(8,128)(2,1)}, bf16[256,2048]{1,0:T(8,128)(2,1)}, u32[]{:S(2)}, u32[]{:S(2)}) collective-permute-start(bf16[256,2048]{1,0:T(8,128)(2,1)} %bitcast.48), channel_id=1, source_target_pairs={{0,8},{16,24},{1,9},{17,25},{2,10},{18,26},{3,11},{19,27},{4,12},{... | collective-permute-start | bytes 3145736 | tf_op jit(solution)/shard_map/ppermute | solution.py:442
  55.2 39.3 %collective-permute-start.13 = (bf16[256,2048]{1,0:T(8,128)(2,1)S(1)}, bf16[256,2048]{1,0:T(8,128)(2,1)}, u32[]{:S(2)}, u32[]{:S(2)}) collective-permute-start(bf16[256,2048]{1,0:T(8,128)(2,1)S(1)} %collective-permute-done.12.refs_1_), channel_id=1, source_target_pairs={{2,0},{4,6},{3,1},{5,7},{10,8},{12,14},{11,9},{13,15},{18,16},{20,... | collective-permute-start | bytes 3145736 | tf_op jit(solution)/shard_map/ppermute | solution.py:442
  58.8 44.2 %collective-permute-start.16 = (bf16[512,1024]{1,0:T(8,128)(2,1)}, bf16[512,1024]{1,0:T(8,128)(2,1)S(1)}, u32[]{:S(2)}, u32[]{:S(2)}) collective-permute-start(bf16[512,1024]{1,0:T(8,128)(2,1)} %constant_dynamic-slice_fusion), channel_id=1, source_target_pairs={{0,2},{6,4},{1,3},{7,5},{8,10},{14,12},{9,11},{15,13},{16,18},{22,... | collective-permute-start | bytes 3145736 | tf_op jit(solution)/shard_map/ppermute | solution.py:442
  63.9 40.7 %collective-permute-start.21 = (bf16[512,1024]{1,0:T(8,128)(2,1)}, bf16[512,1024]{1,0:T(8,128)(2,1)}, u32[]{:S(2)}, u32[]{:S(2)}) collective-permute-start(bf16[512,1024]{1,0:T(8,128)(2,1)} %constant_dynamic-slice_fusion), channel_id=1, source_target_pairs={{2,4},{4,2},{3,5},{5,3},{10,12},{12,10},{11,13},{13,11},{18,20},{2... | collective-permute-start | bytes 3145736 | tf_op jit(solution)/shard_map/ppermute | solution.py:442
  94.6 25.5 %collective-permute-start.5 = (bf16[256,2048]{1,0:T(8,128)(2,1)}, bf16[256,2048]{1,0:T(8,128)(2,1)}, u32[]{:S(2)}, u32[]{:S(2)}) collective-permute-start(bf16[256,2048]{1,0:T(8,128)(2,1)} %copy-done.25), channel_id=1, source_target_pairs={{16,24},{24,16},{17,25},{25,17},{18,26},{26,18},{19,27},{27,19},{2... | collective-permute-start | bytes 3145736 | tf_op jit(solution)/shard_map/ppermute | solution.py:442
  103.0 25.2 %collective-permute-start.14 = (bf16[256,2176]{1,0:T(8,128)(2,1)S(1)}, bf16[256,2176]{1,0:T(8,128)(2,1)S(1)}, u32[]{:S(2)}, u32[]{:S(2)}) collective-permute-start(bf16[256,2176]{1,0:T(8,128)(2,1)S(1)} %cross_attention.6), channel_id=1, source_target_pairs={{0,2},{6,4},{1,3},{7,5},{8,10},{14,12},{9,11},{15,13},{16,18},{22,... | collective-permute-start | bytes 3342344 | tf_op jit(solution)/shard_map/ppermute | solution.py:442
  104.6 39.5 %collective-permute-start.18 = (bf16[512,1024]{1,0:T(8,128)(2,1)S(1)}, bf16[512,1024]{1,0:T(8,128)(2,1)S(1)}, u32[]{:S(2)}, u32[]{:S(2)}) collective-permute-start(bf16[512,1024]{1,0:T(8,128)(2,1)S(1)} %collective-permute-done.16.refs_1_), channel_id=1, source_target_pairs={{0,16},{8,24},{16,0},{24,8},{1,17},{9,25},{17,1},{25,9},{2,18},{10... | collective-permute-start | bytes 3145736 | tf_op jit(solution)/shard_map/ppermute | solution.py:442
  114.8 33.6 %collective-permute-start.19 = (bf16[512,1024]{1,0:T(8,128)(2,1)S(1)}, bf16[512,1024]{1,0:T(8,128)(2,1)S(1)}, u32[]{:S(2)}, u32[]{:S(2)}) collective-permute-start(bf16[512,1024]{1,0:T(8,128)(2,1)S(1)} %collective-permute-done.16.refs_1_), channel_id=1, source_target_pairs={{0,8},{8,0},{16,24},{24,16},{1,9},{9,1},{17,25},{25,17},{2,10},{10... | collective-permute-start | bytes 3145736 | tf_op jit(solution)/shard_map/ppermute | solution.py:442
  114.8 33.7 %collective-permute-start.25 = (bf16[512,1024]{1,0:T(8,128)(2,1)S(1)}, bf16[512,1024]{1,0:T(8,128)(2,1)}, u32[]{:S(2)}, u32[]{:S(2)}) collective-permute-start(bf16[512,1024]{1,0:T(8,128)(2,1)S(1)} %collective-permute-done.16.refs_1_), channel_id=1, source_target_pairs={{2,4},{4,2},{3,5},{5,3},{10,12},{12,10},{11,13},{13,11},{18,20},{2... | collective-permute-start | bytes 3145736 | tf_op jit(solution)/shard_map/ppermute | solution.py:442
  120.1 29.3 %collective-permute-start.17 = (bf16[256,2176]{1,0:T(8,128)(2,1)S(1)}, bf16[256,2176]{1,0:T(8,128)(2,1)S(1)}, u32[]{:S(2)}, u32[]{:S(2)}) collective-permute-start(bf16[256,2176]{1,0:T(8,128)(2,1)S(1)} %cross_attention.8), channel_id=1, source_target_pairs={{0,2},{6,4},{1,3},{7,5},{8,10},{14,12},{9,11},{15,13},{16,18},{22,... | collective-permute-start | bytes 3342344 | tf_op jit(solution)/shard_map/ppermute | solution.py:442
  128.1 35.0 %collective-permute-start.22 = (bf16[512,1024]{1,0:T(8,128)(2,1)}, bf16[512,1024]{1,0:T(8,128)(2,1)}, u32[]{:S(2)}, u32[]{:S(2)}) collective-permute-start(bf16[512,1024]{1,0:T(8,128)(2,1)} %collective-permute-done.21.refs_5_), channel_id=1, source_target_pairs={{0,16},{8,24},{16,0},{24,8},{1,17},{9,25},{17,1},{25,9},{2,18},{10... | collective-permute-start | bytes 3145736 | tf_op jit(solution)/shard_map/ppermute | solution.py:442
  144.1 40.3 %collective-permute-start.31 = (bf16[256,2176]{1,0:T(8,128)(2,1)S(1)}, bf16[256,2176]{1,0:T(8,128)(2,1)S(1)}, u32[]{:S(2)}, u32[]{:S(2)}) collective-permute-start(bf16[256,2176]{1,0:T(8,128)(2,1)S(1)} %cross_attention.7), channel_id=1, source_target_pairs={{0,2},{6,4},{1,3},{7,5},{8,10},{14,12},{9,11},{15,13},{16,18},{22,... | collective-permute-start | bytes 3342344 | tf_op jit(solution)/shard_map/ppermute | solution.py:442
  148.5 35.9 %collective-permute-start.26 = (bf16[512,1024]{1,0:T(8,128)(2,1)}, bf16[512,1024]{1,0:T(8,128)(2,1)}, u32[]{:S(2)}, u32[]{:S(2)}) collective-permute-start(bf16[512,1024]{1,0:T(8,128)(2,1)} %collective-permute-done.25.refs_9_), channel_id=1, source_target_pairs={{0,16},{8,24},{16,0},{24,8},{1,17},{9,25},{17,1},{25,9},{2,18},{10... | collective-permute-start | bytes 3145736 | tf_op jit(solution)/shard_map/ppermute | solution.py:442
  149.4 46.3 %collective-permute-start.15 = (bf16[256,2176]{1,0:T(8,128)(2,1)S(1)}, bf16[256,2176]{1,0:T(8,128)(2,1)S(1)}, u32[]{:S(2)}, u32[]{:S(2)}) collective-permute-start(bf16[256,2176]{1,0:T(8,128)(2,1)S(1)} %cross_attention.7), channel_id=1, source_target_pairs={{2,4},{4,2},{3,5},{5,3},{10,12},{12,10},{11,13},{13,11},{18,20},{2... | collective-permute-start | bytes 3342344 | tf_op jit(solution)/shard_map/ppermute | solution.py:442
  163.1 26.5 %collective-permute-start.23 = (bf16[512,1024]{1,0:T(8,128)(2,1)}, bf16[512,1024]{1,0:T(8,128)(2,1)S(1)}, u32[]{:S(2)}, u32[]{:S(2)}) collective-permute-start(bf16[512,1024]{1,0:T(8,128)(2,1)} %collective-permute-done.21.refs_5_), channel_id=1, source_target_pairs={{0,8},{8,0},{16,24},{24,16},{1,9},{9,1},{17,25},{25,17},{2,10},{10... | collective-permute-start | bytes 3145736 | tf_op jit(solution)/shard_map/ppermute | solution.py:442
  163.1 39.8 %collective-permute-start.27 = (bf16[512,1024]{1,0:T(8,128)(2,1)}, bf16[512,1024]{1,0:T(8,128)(2,1)}, u32[]{:S(2)}, u32[]{:S(2)}) collective-permute-start(bf16[512,1024]{1,0:T(8,128)(2,1)} %collective-permute-done.25.refs_9_), channel_id=1, source_target_pairs={{0,8},{8,0},{16,24},{24,16},{1,9},{9,1},{17,25},{25,17},{2,10},{10... | collective-permute-start | bytes 3145736 | tf_op jit(solution)/shard_map/ppermute | solution.py:442
  189.6 29.4 %collective-permute-start.32 = (bf16[256,2176]{1,0:T(8,128)(2,1)}, bf16[256,2176]{1,0:T(8,128)(2,1)}, u32[]{:S(2)}, u32[]{:S(2)}) collective-permute-start(bf16[256,2176]{1,0:T(8,128)(2,1)} %cross_attention.10), channel_id=1, source_target_pairs={{0,2},{6,4},{1,3},{7,5},{8,10},{14,12},{9,11},{15,13},{16,18},{22,... | collective-permute-start | bytes 3342344 | tf_op jit(solution)/shard_map/ppermute | solution.py:442
  204.6 25.5 %collective-permute-start.29 = (bf16[256,2048]{1,0:T(8,128)(2,1)}, bf16[256,2048]{1,0:T(8,128)(2,1)}, u32[]{:S(2)}, u32[]{:S(2)}) collective-permute-start(bf16[256,2048]{1,0:T(8,128)(2,1)} %project.5), channel_id=1, source_target_pairs={{0,1},{1,0},{2,3},{3,2},{4,5},{5,4},{6,7},{7,6},{8,9},{9,8},{10,11... | collective-permute-start | bytes 3145736 | tf_op jit(solution)/shard_map/ppermute | solution.py:442
  220.6 31.8 %collective-permute-start.34 = (bf16[256,2048]{1,0:T(8,128)(2,1)S(1)}, bf16[256,2048]{1,0:T(8,128)(2,1)S(1)}, u32[]{:S(2)}, u32[]{:S(2)}) collective-permute-start(bf16[256,2048]{1,0:T(8,128)(2,1)S(1)} %project.7), channel_id=1, source_target_pairs={{0,1},{1,0},{2,3},{3,2},{4,5},{5,4},{6,7},{7,6},{8,9},{9,8},{10,11... | collective-permute-start | bytes 3145736 | tf_op jit(solution)/shard_map/ppermute | solution.py:442
  231.7 31.4 %collective-permute-start.30 = (bf16[256,2048]{1,0:T(8,128)(2,1)S(1)}, bf16[256,2048]{1,0:T(8,128)(2,1)S(1)}, u32[]{:S(2)}, u32[]{:S(2)}) collective-permute-start(bf16[256,2048]{1,0:T(8,128)(2,1)S(1)} %add_convert_fusion), channel_id=1, source_target_pairs={{2,0},{4,6},{3,1},{5,7},{10,8},{12,14},{11,9},{13,15},{18,16},{20,... | collective-permute-start | bytes 3145736 | tf_op jit(solution)/shard_map/ppermute | solution.py:442
  (38 other events, 760.3 us)
